TPU v7x, 32 devices: a whole 2x2x4 slice. The times are simulated.
32 devices in a mesh: seq: 8 (over z, y), grp: 4 (over x, core).
Axes of the slice: x: 2, y: 2, z: 4, core: 2. Of those that a mesh axis runs over, the one named last changes fastest.
Arguments:
- tokens: bfloat16 [16, 1024, 1024], P('grp', 'seq'), may hold values from -6 to 6
- segment_ids: int32 [16, 1024], P('grp', 'seq'), may hold values from 0 to 3, never falling along the last dimension, each value on 1 to 512 neighbouring positions
- adapter_ids: int32 [16], P('grp'), may hold values from 0 to 7
- input_weight: bfloat16 [1024, 3072], replicated, may hold values from -0.1875 to 0.1875
- conv_weight: float32 [3, 1024], replicated, may hold values from -3.5 to 3.5
- output_weight: bfloat16 [1024, 1024], replicated, may hold values from -0.1875 to 0.1875
- gate_weight: bfloat16 [1024, 4608], replicated, may hold values from -0.1875 to 0.1875
- up_weight: bfloat16 [1024, 4608], replicated, may hold values from -0.1875 to 0.1875
- down_weight: bfloat16 [4608, 1024], replicated, may hold values from -0.09375 to 0.09375
- norm_one: float32 [1024], replicated, may hold values from 0.5 to 1.5
- norm_two: float32 [1024], replicated, may hold values from 0.5 to 1.5
- cotangent: bfloat16 [16, 1024, 1024], P('grp', 'seq'), may hold values from -6 to 6
- adapter_state: float32 [8, 368640], P('grp'), may hold values from -0.18 to 0.18
- first_moment: float32 [8, 368640], P('grp'), as said below
- second_moment: float32 [8, 368640], P('grp'), as said below
- rate: float32 [1], replicated, may hold values from 0.2 to 0.5
- step: int32 [1], replicated, may hold values from 1 to 8
Outputs:
- output: bfloat16 [16, 1024, 1024], P('grp', 'seq')
- input_grad: bfloat16 [16, 1024, 1024], P('grp', 'seq')
- adapter_state_new: float32 [8, 368640], P('grp')
- adapter_table_new: bfloat16 [8, 368640], replicated
Inputs may be any that keep to these rules, and one draw needn't show every extreme that they name: `segment_ids`: within a sequence the numbers start at 0 and never fall; each document holds 1 to 512 positions. `first_moment`: real values of either sign. `second_moment`: Positive.
All inputs are finite; a program needn't handle non-finite values.
Results may differ from a plain program's by a relative error of at most 0.01.
The roundings to bfloat16 on the way count: a program that leaves them out, or rounds other values in their place, can miss the bound.
Values may be sent and summed in bfloat16 or wider, within the bound.
A program may use at most 192 MiB of HBM per device.

v0:
```python
import jax
import jax.numpy as jnp
from jax import lax
from jax.sharding import PartitionSpec as P

D = 1024
FF = 4608
RANK = 16


EPS = 1e-05
adapter_scale = 2.0
highest = lax.Precision.HIGHEST


def passed_along(value, axis, steps):
    count = lax.axis_size(axis)
    first, last = (max(0, -steps), min(count, count - steps))
    return lax.ppermute(value, axis, [(source, source + steps) for source in range(first, last)])


def unpack(vector):
    shapes = (
        (D, RANK),
        (RANK, 3 * D),
        (D, RANK),
        (RANK, D),
        (D, RANK),
        (RANK, FF),
        (D, RANK),
        (RANK, FF),
        (FF, RANK),
        (RANK, D),
    )
    pieces = []
    offset = 0
    for height, breadth in shapes:
        flat_piece = lax.slice_in_dim(
            vector, offset, offset + height * breadth, axis=vector.ndim - 1
        )
        pieces.append(flat_piece.reshape(vector.shape[:-1] + (height, breadth)))
        offset = offset + height * breadth
    return pieces


def rms_parts(values, norm_gain):
    inverse = lax.rsqrt(jnp.mean(values * values, axis=-1, keepdims=True) + EPS)
    return (values * inverse * norm_gain, inverse)


def rms_back(values, inverse, norm_gain, grad_normed):
    scaled = grad_normed * norm_gain
    return inverse * scaled - values * inverse * inverse * inverse * jnp.mean(
        values * scaled, axis=-1, keepdims=True
    )


def dense_product(input_rows, weight_matrix):
    return jnp.einsum("spk,kn->spn", input_rows, weight_matrix, preferred_element_type=jnp.float32)


def dense_back(output_gradient, weight_matrix):
    return jnp.einsum(
        "spn,kn->spk", output_gradient, weight_matrix, preferred_element_type=jnp.float32
    )


def adapter_down_factor(input_rows, down_piece):
    return jnp.einsum(
        "spk,skr->spr", input_rows, down_piece, preferred_element_type=jnp.float32
    ).astype(jnp.bfloat16)


def adapter_up_factor(middle_rows, up_piece):
    return jnp.einsum("spr,srn->spn", middle_rows, up_piece, preferred_element_type=jnp.float32)


def adapter_backward(input_rows, middle_rows, output_gradient, down_piece, up_piece):
    middle_gradient = adapter_scale * jnp.einsum(
        "spn,srn->spr", output_gradient, up_piece, preferred_element_type=jnp.float32
    )
    grad_inputs = jnp.einsum(
        "spr,skr->spk", middle_gradient, down_piece.astype(jnp.float32), precision=highest
    )
    grad_down = jnp.einsum(
        "spk,spr->skr", input_rows.astype(jnp.float32), middle_gradient, precision=highest
    )
    up_gradient = adapter_scale * jnp.einsum(
        "spr,spn->srn", middle_rows, output_gradient, preferred_element_type=jnp.float32
    )
    return (grad_inputs, grad_down, up_gradient)


def adam_step(state, moment_first, moment_second, grad_sum, rate, step):
    decay_power = jnp.power(jnp.float32(0.5), step[0].astype(jnp.float32))
    correction = 1.0 - decay_power
    moment_one = 0.5 * moment_first + 0.5 * grad_sum
    moment_two = 0.5 * moment_second + 0.5 * grad_sum * grad_sum
    return state - rate[0] * (moment_one / correction) / (jnp.sqrt(moment_two / correction) + 1e-08)


def per_device(
    tokens,
    segment_ids,
    adapter_ids,
    input_weight,
    conv_weight,
    output_weight,
    gate_weight,
    up_weight,
    down_weight,
    norm_one,
    norm_two,
    cotangent,
    adapter_state,
    first_moment,
    second_moment,
    rate,
    step,
):
    table = lax.all_gather(adapter_state.astype(jnp.bfloat16), "grp", axis=0, tiled=True)
    pieces_list = unpack(jnp.take(table, adapter_ids, axis=0))
    positions = tokens.shape[1]
    rows_in = tokens.astype(jnp.float32)
    normed_one, inverse_one = rms_parts(rows_in, norm_one)
    normed_rank_rows = normed_one.astype(jnp.bfloat16)
    input_middle_rows = adapter_down_factor(normed_rank_rows, pieces_list[0])
    projected_rows = dense_product(
        normed_rank_rows, input_weight
    ) + adapter_scale * adapter_up_factor(input_middle_rows, pieces_list[1])
    gate_b = projected_rows[:, :, :D]
    gate_c = projected_rows[:, :, D : 2 * D]
    values_x = projected_rows[:, :, 2 * D :]
    mixed_in = gate_b * values_x
    own_ids = segment_ids.astype(jnp.float32)
    came_rows, came_ids = passed_along((mixed_in[:, -2:, :], own_ids[:, -2:]), "seq", 1)
    extended = jnp.concatenate([came_rows, mixed_in], axis=1)
    extended_ids = jnp.concatenate([came_ids, own_ids], axis=1)
    convolved = conv_weight[2] * mixed_in
    masks = []
    for lag_steps in (1, 2):
        earlier_ids = lax.slice_in_dim(
            extended_ids, 2 - lag_steps, 2 - lag_steps + positions, axis=1
        )
        same_doc = (earlier_ids == own_ids).astype(jnp.float32)[:, :, None]
        masks.append(same_doc)
        earlier = lax.slice_in_dim(extended, 2 - lag_steps, 2 - lag_steps + positions, axis=1)
        convolved = convolved + conv_weight[2 - lag_steps] * same_doc * earlier
    gated_hidden = (gate_c * convolved).astype(jnp.bfloat16)
    output_middle_rows = adapter_down_factor(gated_hidden, pieces_list[2])
    branch_output = dense_product(gated_hidden, output_weight) + adapter_scale * adapter_up_factor(
        output_middle_rows, pieces_list[3]
    )
    hidden_one = rows_in + branch_output
    normed_two, inverse_two = rms_parts(hidden_one, norm_two)
    second_normed_rank_rows = normed_two.astype(jnp.bfloat16)
    gate_middle_rows = adapter_down_factor(second_normed_rank_rows, pieces_list[4])
    up_middle_rows = adapter_down_factor(second_normed_rank_rows, pieces_list[6])
    gate_logits = dense_product(
        second_normed_rank_rows, gate_weight
    ) + adapter_scale * adapter_up_factor(gate_middle_rows, pieces_list[5])
    up_activation = dense_product(
        second_normed_rank_rows, up_weight
    ) + adapter_scale * adapter_up_factor(up_middle_rows, pieces_list[7])
    hidden_rows = (jax.nn.silu(gate_logits) * up_activation).astype(jnp.bfloat16)
    down_middle_rows = adapter_down_factor(hidden_rows, pieces_list[8])
    feedforward_output = dense_product(
        hidden_rows, down_weight
    ) + adapter_scale * adapter_up_factor(down_middle_rows, pieces_list[9])
    output = (hidden_one + feedforward_output).astype(jnp.bfloat16)
    hidden_gradient, down_adapter_first_gradient, down_adapter_second_gradient = adapter_backward(
        hidden_rows, down_middle_rows, cotangent, pieces_list[8], pieces_list[9]
    )
    hidden_gradient = hidden_gradient + dense_back(cotangent, down_weight)
    sigmoid_gate = jax.nn.sigmoid(gate_logits)
    grad_gate = (
        hidden_gradient * up_activation * sigmoid_gate * (1.0 + gate_logits * (1.0 - sigmoid_gate))
    ).astype(jnp.bfloat16)
    up_gradient = (hidden_gradient * gate_logits * sigmoid_gate).astype(jnp.bfloat16)
    second_normed_gradient, gate_adapter_first_gradient, gate_adapter_second_gradient = (
        adapter_backward(
            second_normed_rank_rows, gate_middle_rows, grad_gate, pieces_list[4], pieces_list[5]
        )
    )
    gradient_via_up, up_adapter_first_gradient, up_adapter_second_gradient = adapter_backward(
        second_normed_rank_rows, up_middle_rows, up_gradient, pieces_list[6], pieces_list[7]
    )
    second_normed_gradient = (
        second_normed_gradient
        + gradient_via_up
        + dense_back(grad_gate, gate_weight)
        + dense_back(up_gradient, up_weight)
    )
    grad_hidden_one = cotangent.astype(jnp.float32) + rms_back(
        hidden_one, inverse_two, norm_two, second_normed_gradient
    )
    grad_branch = grad_hidden_one.astype(jnp.bfloat16)
    gated_gradient, output_adapter_first_gradient, output_adapter_second_gradient = (
        adapter_backward(
            gated_hidden, output_middle_rows, grad_branch, pieces_list[2], pieces_list[3]
        )
    )
    gated_gradient = gated_gradient + dense_back(grad_branch, output_weight)
    grad_conv = gated_gradient * gate_c
    grad_c = gated_gradient * convolved
    lag_one = conv_weight[1] * masks[0] * grad_conv
    lag_two = conv_weight[0] * masks[1] * grad_conv
    leaving = jnp.concatenate([lag_two[:, :1], lag_two[:, 1:2] + lag_one[:, :1]], axis=1)
    arriving = passed_along(leaving, "seq", -1)
    grad_mixed = conv_weight[2] * grad_conv
    grad_mixed = grad_mixed + jnp.pad(lag_one[:, 1:], ((0, 0), (0, 1), (0, 0)))
    grad_mixed = grad_mixed + jnp.pad(lag_two[:, 2:], ((0, 0), (0, 2), (0, 0)))
    grad_mixed = grad_mixed + jnp.pad(arriving, ((0, 0), (positions - 2, 0), (0, 0)))
    grad_projected = jnp.concatenate(
        [grad_mixed * values_x, grad_c, grad_mixed * gate_b], axis=2
    ).astype(jnp.bfloat16)
    first_normed_gradient, input_adapter_first_gradient, input_adapter_second_gradient = (
        adapter_backward(
            normed_rank_rows, input_middle_rows, grad_projected, pieces_list[0], pieces_list[1]
        )
    )
    first_normed_gradient = first_normed_gradient + dense_back(grad_projected, input_weight)
    input_grad = (
        grad_hidden_one + rms_back(rows_in, inverse_one, norm_one, first_normed_gradient)
    ).astype(jnp.bfloat16)
    pieces = (
        input_adapter_first_gradient,
        input_adapter_second_gradient,
        output_adapter_first_gradient,
        output_adapter_second_gradient,
        gate_adapter_first_gradient,
        gate_adapter_second_gradient,
        up_adapter_first_gradient,
        up_adapter_second_gradient,
        down_adapter_first_gradient,
        down_adapter_second_gradient,
    )
    per_sequence = jnp.concatenate(
        [tensor_part.reshape(tensor_part.shape[0], -1) for tensor_part in pieces], axis=1
    )
    selector = (
        adapter_ids[:, None] == jnp.arange(table.shape[0], dtype=jnp.int32)[None, :]
    ).astype(jnp.float32)
    local_grad = jnp.einsum("sa,sq->aq", selector, per_sequence, precision=highest)
    summed = lax.psum(local_grad, "seq")
    owned = lax.psum_scatter(summed, "grp", scatter_dimension=0, tiled=True)
    fresh = adam_step(adapter_state, first_moment, second_moment, owned, rate, step)
    table_new = lax.all_gather(fresh.astype(jnp.bfloat16), "grp", axis=0, tiled=True)
    return (output, input_grad, fresh, table_new)


def solution(mesh):
    placed = (
        P("grp", "seq", None),
        P("grp", "seq"),
        P("grp"),
        P(),
        P(),
        P(),
        P(),
        P(),
        P(),
        P(),
        P(),
        P("grp", "seq", None),
        P("grp", None),
        P("grp", None),
        P("grp", None),
        P(),
        P(),
    )
    return jax.shard_map(
        per_device,
        mesh=mesh,
        in_specs=placed,
        out_specs=(P("grp", "seq", None), P("grp", "seq", None), P("grp", None), P()),
        check_vma=False,
    )
```

profile of v0, /device:TPU:0, one launch (start us, length us, event | category | flops | bytes accessed | tf_op | source)
XLA Modules:
  0.0 712.3 jit_solution(15527612662962662814)
XLA Ops:
  11.8 4.9 collective-permute-start
  17.1 9.3 %fusion.14 = f32[4,128,3072]{2,1,0:T(8,128)} fusion(bf16[1024,3072]{1,0:T(8,128)(2,1)} %param.20, bf16[4,128,1024]{2,1,0:T(8,128)(2,1)} %param.17, f32[1024]{0:T(1024)S(1)} %copy-done.61, f32[4,128]{1,0:T(4,128)S(1)} %add_rsqrt_fusion.1), kind=kOutput, calls=%fused_computation.24 | convolution fusion | flops 3223322624 | bytes 13637632 | tf_op jit(solution)/shard_map/spk,kn->spn/dot_general | solution.py:59
  26.5 11.4 %fusion = f32[4,128,4608]{2,1,0:T(8,128)} fusion(bf16[4,128,1024]{2,1,0:T(8,128)(2,1)S(1)} %copy-done.7, bf16[4608,1024]{1,0:T(8,128)(2,1)} %param.25), kind=kOutput, calls=%fused_computation.3 | convolution fusion | flops 4831838208 | bytes 19922944 | tf_op jit(solution)/shard_map/spn,kn->spk/dot_general | solution.py:63
  38.5 20.1 %all-gather.5.cloned.1.call-done = bf16[4,2,368640]{2,1,0:T(2,128)(2,1)} async-done(((bf16[1,2,368640]{2,1,0:T(2,128)(2,1)}), bf16[4,2,368640]{2,1,0:T(2,128)(2,1)}) %all-gather.5.cloned.1.call-update) | async-done | bytes 5898256 | tf_op jit(solution)/shard_map/all_gather | solution.py:121
  58.7 7.5 %reshape.158 = bf16[8,368640]{1,0:T(8,128)(2,1)} reshape(bf16[4,2,368640]{2,1,0:T(2,128)(2,1)} %all-gather.5.cloned.1.call-done) | data formatting | bytes 11796480
  66.2 5.4 fusion.81
  71.6 5.0 gather_fusion
  76.6 5.0 gather_fusion.1
  81.5 5.0 gather_fusion.2
  86.5 8.7 %maximum_select_fusion = bf16[4,368640]{1,0:T(4,128)(2,1)S(1)} fusion(bf16[4,122880]{1,0:T(4,128)(2,1)} %gather_fusion.2, bf16[4,122880]{1,0:T(4,128)(2,1)} %gather_fusion.1, bf16[4,122880]{1,0:T(4,128)(2,1)} %gather_fusion, pred[4]{0:T(512)(128)(4,1)S(1)} %compare_and_fusion), kind=kLoop, calls=%fused_computation.47 | loop fusion | flops 10321920 | bytes 5898244 | tf_op jit(solution)/shard_map/jit(_take)/select_n | solution.py:122
  111.2 4.4 collective-permute-start.1
  116.6 6.8 reshape.118
  123.5 13.2 %convolution_add_fusion = f32[4,128,4608]{2,1,0:T(8,128)} fusion(f32[4,128,4608]{2,1,0:T(8,128)} %fusion, f32[4,16,128]{2,1,0:T(8,128)} %convolution_multiply_fusion.9, bf16[4,4608,16]{2,1,0:T(8,128)(2,1)} %reshape.118), kind=kOutput, calls=%fused_computation.21 | convolution fusion | flops 455344128 | bytes 19496960 | tf_op jit(solution)/shard_map/spr,skr->spk/dot_general | solution.py:82
  141.9 6.1 multiply_convert_fusion.7
  153.7 7.8 %fusion.6 = f32[4,128,4608]{2,1,0:T(8,128)S(1)} fusion(bf16[4,128,1024]{2,1,0:T(8,128)(2,1)S(1)} %multiply_convert_fusion.6, bf16[1024,4608]{1,0:T(8,128)(2,1)} %param.24), kind=kOutput, calls=%fused_computation.9 | convolution fusion | flops 4831838208 | bytes 19922944 | tf_op jit(solution)/shard_map/spk,kn->spn/dot_general | solution.py:59
  161.6 7.4 %fusion.10 = f32[4,128,4608]{2,1,0:T(8,128)} fusion(bf16[4,128,1024]{2,1,0:T(8,128)(2,1)S(1)} %multiply_convert_fusion.6, bf16[1024,4608]{1,0:T(8,128)(2,1)S(1)} %bitcast.173), kind=kOutput, calls=%fused_computation.13 | convolution fusion | flops 4831838208 | bytes 19922944 | tf_op jit(solution)/shard_map/spk,kn->spn/dot_general | solution.py:59
  169.0 5.0 multiply_add_fusion
  174.0 15.5 %multiply_convert_fusion.1 = (bf16[4,128,4608]{2,1,0:T(8,128)(2,1)}, bf16[4,128,4608]{2,1,0:T(8,128)(2,1)}, bf16[4,128,4608]{2,1,0:T(8,128)(2,1)}) fusion(f32[4,128,4608]{2,1,0:T(8,128)} %convolution_add_fusion, f32[4,128,4608]{2,1,0:T(8,128)} %multiply_add_fusion, f32[4,128,4608]{2,1,0:T(8,128)} %fusion.10, ...), kind=kOutput, calls=%fused_computation.16 | convolution fusion | flops 117964800 | bytes 43073536 | tf_op jit(solution)/shard_map/spr,srn->spn/dot_general | solution.py:75
  201.4 7.7 %fusion.4 = f32[4,128,1024]{2,1,0:T(8,128)S(1)} fusion(bf16[4,128,4608]{2,1,0:T(8,128)(2,1)S(1)} %bitcast.146, bf16[1024,4608]{1,0:T(8,128)(2,1)} %param.24), kind=kOutput, calls=%fused_computation.7 | convolution fusion | flops 4831838208 | bytes 16252928 | tf_op jit(solution)/shard_map/spn,kn->spk/dot_general | solution.py:63
  209.1 8.1 %fusion.8 = f32[4,128,1024]{2,1,0:T(8,128)S(1)} fusion(bf16[4,128,4608]{2,1,0:T(8,128)(2,1)S(1)} %bitcast.148, bf16[1024,4608]{1,0:T(8,128)(2,1)} %param.23), kind=kOutput, calls=%fused_computation.11 | convolution fusion | flops 4831838208 | bytes 16252928 | tf_op jit(solution)/shard_map/spn,kn->spk/dot_general | solution.py:63
  226.1 7.0 fusion.91
  263.0 9.6 %reshape.128 = f32[4,73728]{1,0:T(4,128)} reshape(f32[4,4608,16]{2,1,0:T(8,128)} %fusion.91) | data formatting | bytes 2359296 | tf_op jit(solution)/shard_map/reshape | solution.py:239
  273.4 5.0 multiply_convert_fusion.5
  293.5 9.5 %fusion.73 = f32[8,368640]{1,0:T(8,128)} fusion(f32[4,368640]{1,0:T(4,128)S(1)} %constant_dynamic-update-slice_fusion, s32[4]{0:T(128)S(1)} %copy-done.65), kind=kOutput, calls=%fused_computation.145 | convolution fusion | flops 141557792 | bytes 17694736 | tf_op jit(solution)/shard_map/sa,sq->aq/dot_general | solution.py:244
  305.0 207.4 %all-reduce.9.cloned.1.call-done = f32[8,368640]{1,0:T(8,128)} async-done(((f32[8,368640]{1,0:T(8,128)}), f32[8,368640]{1,0:T(8,128)}) %all-reduce.9.cloned.1.call-update) | async-done | bytes 11796496
  512.4 6.8 constant_dynamic-slice_fusion
  520.8 122.3 %all-reduce.7.cloned.1.call-done = f32[2,368640]{1,0:T(2,128)} async-done(((f32[2,368640]{1,0:T(2,128)}), f32[2,368640]{1,0:T(2,128)}) %all-reduce.7.cloned.1.call-update) | async-done | bytes 2949136 | tf_op jit(solution)/shard_map/psum | solution.py:245
  643.1 11.2 %convert_bitcast_fusion = (bf16[1,2,368640]{2,1,0:T(2,128)(2,1)}, f32[2,368640]{1,0:T(2,128)}) fusion(f32[2,368640]{1,0:T(2,128)} %param.29, f32[2,368640]{1,0:T(2,128)} %all-reduce.7.cloned.1.call-done, f32[2,368640]{1,0:T(2,128)} %param.31, f32[]{:T(128)} %bitcast.10, f32[2,368640]{1,0:T(2,128)} %param.30, f32[]{:T(128)} %bitcast.142), kind=kLoop, calls=%fused_computation.84 | loop fusion | flops 9584640 | bytes 16220168
  654.4 9.1 %fusion.2 = f32[4,128,1024]{2,1,0:T(8,128)S(1)} fusion(bf16[4,128,4608]{2,1,0:T(8,128)(2,1)} %get-tuple-element.11, bf16[4608,1024]{1,0:T(8,128)(2,1)} %param.25), kind=kOutput, calls=%fused_computation.5 | convolution fusion | flops 4831838208 | bytes 16252928 | tf_op jit(solution)/shard_map/spk,kn->spn/dot_general | solution.py:59
  666.2 6.6 fusion.34
  674.5 23.2 %all-gather.7.cloned.1.call-done = bf16[4,2,368640]{2,1,0:T(2,128)(2,1)} async-done(((bf16[1,2,368640]{2,1,0:T(2,128)(2,1)}), bf16[4,2,368640]{2,1,0:T(2,128)(2,1)}) %all-gather.7.cloned.1.call-update) | async-done | bytes 5898256 | tf_op jit(solution)/shard_map/all_gather | solution.py:248
  697.7 7.6 %reshape.160 = bf16[8,368640]{1,0:T(8,128)(2,1)} reshape(bf16[4,2,368640]{2,1,0:T(2,128)(2,1)} %all-gather.7.cloned.1.call-done) | data formatting | bytes 11796480
  (252 shorter events, 105.4 us)
Async XLA Ops:
  7.2 141.8 %copy-start = (bf16[1024,1024]{1,0:T(8,128)(2,1)S(1)}, bf16[1024,1024]{1,0:T(8,128)(2,1)}, u32[]{:S(2)}) copy-start(bf16[1024,1024]{1,0:T(8,128)(2,1)} %param.22) | copy-start | bytes 6291460
  7.2 9.5 %copy-start.64 = (s32[4]{0:T(128)S(1)}, s32[4]{0:T(128)}, u32[]{:S(2)}) copy-start(s32[4]{0:T(128)} %param.19) | copy-start | bytes 52
  7.2 9.5 %copy-start.14 = (bf16[4,128,1024]{2,1,0:T(8,128)(2,1)S(1)}, bf16[4,128,1024]{2,1,0:T(8,128)(2,1)}, u32[]{:S(2)}) copy-start(bf16[4,128,1024]{2,1,0:T(8,128)(2,1)} %param.17) | copy-start | bytes 3145732
  7.2 9.8 %copy-start.60 = (f32[3,1024]{1,0:T(4,128)S(1)}, f32[3,1024]{1,0:T(4,128)}, u32[]{:S(2)}) copy-start(f32[3,1024]{1,0:T(4,128)} %param.21) | copy-start | bytes 36868
  7.2 9.9 %copy-start.61 = (f32[1024]{0:T(1024)S(1)}, f32[1024]{0:T(1024)}, u32[]{:S(2)}) copy-start(f32[1024]{0:T(1024)} %param.26) | copy-start | bytes 12292
  7.2 51.4 %all-gather.5.cloned.1.call-start = ((), (), s32[]{:S(2)}) async-start(), calls=%async_computation.1 | async-start | bytes 7372800 | tf_op jit(solution)/shard_map/all_gather | solution.py:121
  11.7 500.7 %all-reduce.9.cloned.1.call-start = ((), (), s32[]{:S(2)}) async-start(), calls=%async_computation.3 | async-start | bytes 23592960
  11.8 26.1 %collective-permute-start = (f32[4,2]{1,0:T(4,128)S(1)}, f32[4,2]{1,0:T(4,128)S(1)}, u32[]{:S(2)}, u32[]{:S(2)}) collective-permute-start(f32[4,2]{1,0:T(4,128)S(1)} %slice.91), channel_id=1, source_target_pairs={{0,4},{4,8},{8,12},{12,16},{16,20},{20,24},{24,28},{1,5},{5,9},{9,... | collective-permute-start | bytes 104 | tf_op jit(solution)/shard_map/ppermute | solution.py:19
  17.1 9.4 %copy-start.55 = (f32[4,128]{1,0:T(4,128)}, f32[4,128]{1,0:T(4,128)S(1)}, u32[]{:S(2)}) copy-start(f32[4,128]{1,0:T(4,128)S(1)} %add_rsqrt_fusion.1) | copy-start | bytes 6148
  17.1 124.8 %copy-start.46 = (f32[1,1024]{1,0:T(1,128)}, f32[1,1024]{1,0:T(1,128)S(1)}, u32[]{:S(2)}) copy-start(f32[1,1024]{1,0:T(1,128)S(1)} %get-tuple-element.30) | copy-start | bytes 12292
  17.1 124.7 %copy-start.48 = (f32[1,1024]{1,0:T(1,128)}, f32[1,1024]{1,0:T(1,128)S(1)}, u32[]{:S(2)}) copy-start(f32[1,1024]{1,0:T(1,128)S(1)} %get-tuple-element.31) | copy-start | bytes 12292
  17.1 124.7 %copy-start.50 = (f32[1,1024]{1,0:T(1,128)}, f32[1,1024]{1,0:T(1,128)S(1)}, u32[]{:S(2)}) copy-start(f32[1,1024]{1,0:T(1,128)S(1)} %get-tuple-element.32) | copy-start | bytes 12292
  17.1 9.3 %copy-start.7 = (bf16[4,128,1024]{2,1,0:T(8,128)(2,1)S(1)}, bf16[4,128,1024]{2,1,0:T(8,128)(2,1)}, u32[]{:S(2)}) copy-start(bf16[4,128,1024]{2,1,0:T(8,128)(2,1)} %param.28) | copy-start | bytes 3145732
  38.5 103.3 %copy-start.52 = (f32[4,128]{1,0:T(4,128)}, f32[4,128]{1,0:T(4,128)S(1)}, u32[]{:S(2)}) copy-start(f32[4,128]{1,0:T(4,128)S(1)} %get-tuple-element.33) | copy-start | bytes 6148
  107.3 8.4 %copy-start.30 = (bf16[4,16384]{1,0:T(4,128)(2,1)S(1)}, bf16[4,16384]{1,0:T(4,128)(2,1)}, u32[]{:S(2)}) copy-start(bf16[4,16384]{1,0:T(4,128)(2,1)} %get-tuple-element.18) | copy-start | bytes 393220
  111.2 30.6 %collective-permute-start.1 = (f32[4,2,1024]{2,1,0:T(2,128)}, f32[4,2,1024]{2,1,0:T(2,128)}, u32[]{:S(2)}, u32[]{:S(2)}) collective-permute-start(f32[4,2,1024]{2,1,0:T(2,128)} %slice.124), channel_id=1, source_target_pairs={{0,4},{4,8},{8,12},{12,16},{16,20},{20,24},{24,28},{1,5},{5,9},{9,... | collective-permute-start | bytes 98312 | tf_op jit(solution)/shard_map/ppermute | solution.py:19
  123.5 13.2 %copy-start.44 = (bf16[4,16384]{1,0:T(4,128)(2,1)S(1)}, bf16[4,16384]{1,0:T(4,128)(2,1)}, u32[]{:S(2)}) copy-start(bf16[4,16384]{1,0:T(4,128)(2,1)} %get-tuple-element.22) | copy-start | bytes 393220
  123.5 14.9 %copy-start.43 = (bf16[4,16384]{1,0:T(4,128)(2,1)S(1)}, bf16[4,16384]{1,0:T(4,128)(2,1)}, u32[]{:S(2)}) copy-start(bf16[4,16384]{1,0:T(4,128)(2,1)} %get-tuple-element.20) | copy-start | bytes 393220
  123.5 16.7 %copy-start.42 = (bf16[4,16384]{1,0:T(4,128)(2,1)S(1)}, bf16[4,16384]{1,0:T(4,128)(2,1)}, u32[]{:S(2)}) copy-start(bf16[4,16384]{1,0:T(4,128)(2,1)} %get-tuple-element.19) | copy-start | bytes 393220
  150.7 68.4 %copy-start.3 = (f32[4,128,1024]{2,1,0:T(8,128)}, f32[4,128,1024]{2,1,0:T(8,128)S(1)}, u32[]{:S(2)}) copy-start(f32[4,128,1024]{2,1,0:T(8,128)S(1)} %get-tuple-element.36) | copy-start | bytes 6291460
  152.7 8.9 %slice-start.8 = ((s8[9437184]{0:T(1024)(128)(4,1)}), s8[4194304]{0:T(1024)(128)(4,1)S(1)}, s32[]{:S(2)}) async-start(s8[9437184]{0:T(1024)(128)(4,1)} %bitcast.172), calls=%async_computation.12 | async-start | bytes 8388608
  189.5 10.5 %slice-start.2 = ((s8[4718592]{0:T(1024)(128)(4,1)}), s8[4194304]{0:T(1024)(128)(4,1)S(1)}, s32[]{:S(2)}) async-start(s8[4718592]{0:T(1024)(128)(4,1)} %bitcast.145), calls=%async_computation.6 | async-start | bytes 8388608
  200.1 9.0 %slice-start.4 = ((s8[4718592]{0:T(1024)(128)(4,1)}), s8[4194304]{0:T(1024)(128)(4,1)S(1)}, s32[]{:S(2)}) async-start(s8[4718592]{0:T(1024)(128)(4,1)} %bitcast.147), calls=%async_computation.8 | async-start | bytes 8388608
  209.1 8.1 %copy-start.11 = (bf16[4,1024,16]{2,1,0:T(8,128)(2,1)S(1)}, bf16[4,1024,16]{2,1,0:T(8,128)(2,1)}, u32[]{:S(2)}) copy-start(bf16[4,1024,16]{2,1,0:T(8,128)(2,1)} %reshape.116) | copy-start | bytes 393220
  224.3 8.8 %slice-start = ((s8[4718592]{0:T(1024)(128)(4,1)}), s8[4194304]{0:T(1024)(128)(4,1)S(1)}, s32[]{:S(2)}) async-start(s8[4718592]{0:T(1024)(128)(4,1)} %bitcast.143), calls=%async_computation.4 | async-start | bytes 8388608
  242.7 30.7 %collective-permute-start.2 = (f32[4,2,1024]{2,1,0:T(2,128)}, f32[4,2,1024]{2,1,0:T(2,128)}, u32[]{:S(2)}, u32[]{:S(2)}) collective-permute-start(f32[4,2,1024]{2,1,0:T(2,128)} %pad_maximum_fusion.2), channel_id=1, source_target_pairs={{4,0},{8,4},{12,8},{16,12},{20,16},{24,20},{28,24},{5,1},{9,5},{13... | collective-permute-start | bytes 98312 | tf_op jit(solution)/shard_map/ppermute | solution.py:19
  263.0 9.6 %copy-start.41 = (f32[1,4,16,1024]{3,2,1,0:T(8,128)S(1)}, f32[1,4,16,1024]{3,2,1,0:T(8,128)}, u32[]{:S(2)}) copy-start(f32[1,4,16,1024]{3,2,1,0:T(8,128)} %fusion.43) | copy-start | bytes 786436
  263.0 10.4 %copy-start.47 = (f32[1,1024]{1,0:T(1,128)S(1)}, f32[1,1024]{1,0:T(1,128)}, u32[]{:S(2)}) copy-start(f32[1,1024]{1,0:T(1,128)} %copy-done.46) | copy-start | bytes 12292
  303.1 340.0 %all-reduce.7.cloned.1.call-start = ((), (), s32[]{:S(2)}) async-start(), calls=%async_computation | async-start | bytes 5898240 | tf_op jit(solution)/shard_map/psum | solution.py:245
  519.2 178.5 %all-gather.7.cloned.1.call-start = ((), (), s32[]{:S(2)}) async-start(), calls=%async_computation.2 | async-start | bytes 7372800 | tf_op jit(solution)/shard_map/all_gather | solution.py:248
  654.4 9.2 %copy-start.4 = (f32[4,128,1024]{2,1,0:T(8,128)S(1)}, f32[4,128,1024]{2,1,0:T(8,128)}, u32[]{:S(2)}) copy-start(f32[4,128,1024]{2,1,0:T(8,128)} %copy-done.3) | copy-start | bytes 6291460
  654.4 9.2 %copy-start.31 = (bf16[4,16384]{1,0:T(4,128)(2,1)S(1)}, bf16[4,16384]{1,0:T(4,128)(2,1)}, u32[]{:S(2)}) copy-start(bf16[4,16384]{1,0:T(4,128)(2,1)} %get-tuple-element.18) | copy-start | bytes 393220
  (53 other events, 189.6 us)
Sparse Core Ops, SparseCore 0:
  11.8 46.8 all-gather.4
  303.2 209.1 all-reduce.8
  519.3 123.7 all-reduce.6
  654.5 43.1 all-gather.6
where the time goes:
time: 716 us; the launch traced here: 712 us
  waiting for transfers between devices  373 us (52%)
  matrix products  160 us (22%)
  local copies, waits for them, and re-layouts  105 us (15%)
  other arithmetic  45.6 us (6%)
  between operations  17.2 us (2%)
  starting transfers between devices  11.1 us (2%)
    unnamed x5, waiting for transfers between devices  207 us
    psum x1, waiting for transfers between devices, per_device(): summed = lax.psum(local_grad, 'seq')  122 us
    unnamed x174, local copies, waits for them, and re-layouts  42.1 us
    dot_general x5, matrix products, dense_product(): jnp.einsum('spk,kn->spn', input_rows, weight_matrix, preferred_element_ty...  35.2 us
    dot_general x5, matrix products, dense_back(): jnp.einsum('spn,kn->spk', output_gradient, weight_matrix, preferred_eleme...  35.2 us
    dot_general x5, matrix products, adapter_up_factor(): jnp.einsum('spr,srn->spn', middle_rows, up_piece, preferred_element_type=...  26.2 us
    all_gather x1, waiting for transfers between devices, per_device(): lax.all_gather(fresh.astype(jnp.bfloat16), 'grp', axis=0, tiled=True)  23.2 us
    reshape x5, local copies, waits for them, and re-layouts, per_device(): tensor_part.reshape(tensor_part.shape[0], -1)  21.6 us
  transfers between devices with their start and end apart: 7, of which 4 were waited for; matrix products, arithmetic and copies ran while one was open for 14% of the time, Pallas kernels for 0%

commit v1 on v0

v1 whole, which is shorter than its diff:
```python
import functools

import jax
import jax.numpy as jnp
from jax import lax
from jax.experimental import pallas as pl
from jax.experimental.pallas import tpu as pltpu
from jax.sharding import PartitionSpec as P

D = 1024
FF = 4608
RANK = 16
EPS = 1e-05
FB = 512
MIB = 2**20

f32 = jnp.float32
bf16 = jnp.bfloat16
MESH = pl.DeviceIdType.MESH

WIRE = RANK * 0 + 23040
PACKROWS = 2880
A_IN, B_IN, A_OUT, B_OUT, A_GATE, B_GATE, A_UP, B_UP, A_DOWN, B_DOWN = (
    0, 1024, 4096, 5120, 6144, 7168, 11776, 12800, 17408, 22016,
)
B_PARTS = ((B_IN, 3 * D), (B_OUT, D), (B_GATE, FF), (B_UP, FF), (B_DOWN, D))
A_PARTS = ((A_IN, D), (A_OUT, D), (A_GATE, D), (A_UP, D), (A_DOWN, FF))
A_CHUNKS = tuple(
    (first + start, min(1024, height - start))
    for first, height in A_PARTS
    for start in range(0, height, 1024)
)


def dot(a, b):
    return jnp.dot(a, b, preferred_element_type=f32)


def dot_nt(a, b):
    return lax.dot_general(a, b, (((1,), (1,)), ((), ())), preferred_element_type=f32)


def dot_tn(a, b):
    return lax.dot_general(a, b, (((0,), (0,)), ((), ())), preferred_element_type=f32)


def shuffle_matrix():
    row = lax.broadcasted_iota(jnp.int32, (1024, 1024), 0)
    col = lax.broadcasted_iota(jnp.int32, (1024, 1024), 1)
    return jnp.where(col == 8 * (row % 128) + row // 128, 1.0, 0.0).astype(bf16)


def table_kernel(na, st_ref, out_ref, lhs_ref):
    for n, (first, count) in enumerate(A_CHUNKS):
        for a in range(na):
            packed = st_ref[pl.ds(na * (first // 8) + a, 128, stride=na), :]
            turned = packed.T.astype(bf16)
            row = (n * na + a) * RANK
            for c in range(8):
                lhs_ref[row : row + RANK, 128 * c : 128 * c + 128] = turned[RANK * c : RANK * c + RANK, :]
    full = dot(lhs_ref[...], shuffle_matrix()).astype(bf16)
    for n, (first, count) in enumerate(A_CHUNKS):
        for a in range(na):
            row = (n * na + a) * RANK
            out_ref[a * RANK : (a + 1) * RANK, first : first + count] = full[row : row + RANK, :count]
    for first, breadth in B_PARTS:
        blocks = breadth // 128
        for a in range(na):
            for c in range(blocks):
                part = st_ref[pl.ds(na * (first // 8 + c) + a, RANK, stride=na * blocks), :]
                out_ref[a * RANK : (a + 1) * RANK, first + 128 * c : first + 128 * c + 128] = part.astype(bf16)


def build_table(state_native, na):
    return pl.pallas_call(
        functools.partial(table_kernel, na),
        out_shape=jax.ShapeDtypeStruct((na * RANK, WIRE), bf16),
        scratch_shapes=[pltpu.VMEM((len(A_CHUNKS) * na * RANK, 1024), bf16)],
        compiler_params=pltpu.CompilerParams(vmem_limit_bytes=40 * MIB),
    )(state_native)


def adam_kernel(na, scal_ref, gw_ref, st_ref, m_ref, v_ref, new_ref, tab_ref, lhs_ref, gn_ref):
    for n, (first, count) in enumerate(A_CHUNKS):
        for a in range(na):
            row = (n * na + a) * RANK
            lhs_ref[row : row + RANK, :] = gw_ref[a * RANK : (a + 1) * RANK, first : first + 1024].astype(bf16)
    full = dot_nt(lhs_ref[...], shuffle_matrix())
    for n, (first, count) in enumerate(A_CHUNKS):
        for a in range(na):
            row = (n * na + a) * RANK
            turned = jnp.concatenate(
                [full[row : row + RANK, 128 * c : 128 * c + 128] for c in range(8)], axis=0
            )
            gn_ref[pl.ds(na * (first // 8) + a, count // 8, stride=na), :] = turned.T[: count // 8]
    for first, breadth in B_PARTS:
        blocks = breadth // 128
        for a in range(na):
            for c in range(blocks):
                gn_ref[pl.ds(na * (first // 8 + c) + a, RANK, stride=na * blocks), :] = gw_ref[
                    a * RANK : (a + 1) * RANK, first + 128 * c : first + 128 * c + 128
                ].astype(f32)
    rate = scal_ref[0]
    inv = scal_ref[1]
    grad = gn_ref[...]
    one = 0.5 * m_ref[...] + 0.5 * grad
    two = 0.5 * v_ref[...] + 0.5 * grad * grad
    new = st_ref[...] - rate * (one * inv) / (jnp.sqrt(two * inv) + 1e-08)
    new_ref[...] = new
    tab_ref[...] = new.astype(bf16)


def adam(scal, gw, st, m, v, na):
    rows = na * PACKROWS
    vm = pl.BlockSpec(memory_space=pltpu.VMEM)
    return pl.pallas_call(
        functools.partial(adam_kernel, na),
        in_specs=[pl.BlockSpec(memory_space=pltpu.SMEM)] + [vm] * 4,
        out_shape=(jax.ShapeDtypeStruct((rows, 128), f32), jax.ShapeDtypeStruct((rows, 128), bf16)),
        scratch_shapes=[
            pltpu.VMEM((len(A_CHUNKS) * na * RANK, 1024), bf16),
            pltpu.VMEM((rows, 128), f32),
        ],
        compiler_params=pltpu.CompilerParams(vmem_limit_bytes=56 * MIB),
    )(scal, gw, st, m, v)


def greet(seq, count):
    barrier = pltpu.get_barrier_semaphore()

    @pl.when(seq > 0)
    def _():
        pl.semaphore_signal(barrier, inc=1, device_id={"seq": seq - 1}, device_id_type=MESH)

    @pl.when(seq < count - 1)
    def _():
        pl.semaphore_signal(barrier, inc=1, device_id={"seq": seq + 1}, device_id_type=MESH)

    before = (seq + count - 1) // count
    after = (2 * count - 2 - seq) // count
    pl.semaphore_wait(barrier, before + after)


def row_mask(mask_ref, seqs, length):
    return jnp.concatenate(
        [jnp.broadcast_to(mask_ref[s : s + 1, :], (length, 128)) for s in range(seqs)], axis=0
    )


def norm(values, gain):
    inverse = lax.rsqrt(jnp.mean(values * values, axis=-1, keepdims=True) + EPS)
    return values * inverse * gain, inverse


def pre_kernel(
    seqs, length, count,
    tok_ref, ids_ref, mask_ref, tb_ref, wi_ref, cw_ref, wo_ref, n1_ref, n2_ref, cot_ref,
    u1_ref, mi_ref, b_ref, c_ref, x_ref, conv_ref, same_ref, gated_ref, mo_ref, h1_ref, u2_ref, mg_ref, mu_ref, gd_ref,
    ext_ref, out_ref, in_ref, send_sem, recv_sem,
):
    seq = lax.axis_index("seq")
    greet(seq, count)
    mask = row_mask(mask_ref, seqs, length)
    twice = 2.0 * mask
    tokens = tok_ref[...].astype(f32)
    u1 = norm(tokens, n1_ref[...])[0].astype(bf16)
    u1_ref[...] = u1
    mid = (dot_nt(u1, tb_ref[:, A_IN : A_IN + D]).astype(bf16).astype(f32) * twice).astype(bf16)
    mi_ref[...] = mid
    for third, to_ref in ((0, b_ref), (2, x_ref)):
        for k in range(2):
            col = third * D + 512 * k
            to_ref[:, 512 * k : 512 * k + 512] = dot(u1, wi_ref[:, col : col + 512]) + dot(
                mid, tb_ref[:, B_IN + col : B_IN + col + 512]
            )
    width = D + 128
    for s in range(seqs):
        rows = pl.ds(s * length, length)
        ext_ref[s, 0:8, :] = jnp.zeros((8, width), f32)
        ext_ref[s, 8:, :D] = b_ref[rows, :] * x_ref[rows, :]
        ext_ref[s, 8:, D:] = jnp.broadcast_to(ids_ref[s : s + 1, :], (length, 128)).T
        out_ref[2 * s : 2 * s + 2, :] = ext_ref[s, length + 6 : length + 8, :]
    along = pltpu.make_async_remote_copy(
        src_ref=out_ref, dst_ref=in_ref, send_sem=send_sem, recv_sem=recv_sem,
        device_id={"seq": seq + 1}, device_id_type=MESH,
    )

    @pl.when(seq < count - 1)
    def _():
        along.start()

    for k in range(2):
        col = D + 512 * k
        c_ref[:, 512 * k : 512 * k + 512] = dot(u1, wi_ref[:, col : col + 512]) + dot(
            mid, tb_ref[:, B_IN + col : B_IN + col + 512]
        )
    gd_ref[...] = (dot_nt(cot_ref[...], tb_ref[:, B_DOWN : B_DOWN + D]) * twice).astype(bf16)

    @pl.when(seq < count - 1)
    def _():
        along.wait_send()

    @pl.when(seq > 0)
    def _():
        along.wait_recv()
        for s in range(seqs):
            ext_ref[s, 6:8, :] = in_ref[2 * s : 2 * s + 2, :]

    for s in range(seqs):
        rows = pl.ds(s * length, length)
        now_ids = ext_ref[s, 8:, D:]
        same1 = jnp.where(ext_ref[s, pl.ds(7, length), D:] == now_ids, 1.0, 0.0)
        same2 = jnp.where(ext_ref[s, pl.ds(6, length), D:] == now_ids, 1.0, 0.0)
        same_ref[0, rows, :] = same1
        same_ref[1, rows, :] = same2
        conv = (
            cw_ref[2:3, :] * ext_ref[s, 8:, :D]
            + cw_ref[1:2, :] * same1[:, :1] * ext_ref[s, pl.ds(7, length), :D]
            + cw_ref[0:1, :] * same2[:, :1] * ext_ref[s, pl.ds(6, length), :D]
        )
        conv_ref[rows, :] = conv
        gated_ref[rows, :] = (c_ref[rows, :] * conv).astype(bf16)
    gated = gated_ref[...]
    mid_out = (dot_nt(gated, tb_ref[:, A_OUT : A_OUT + D]).astype(bf16).astype(f32) * twice).astype(bf16)
    mo_ref[...] = mid_out
    for k in range(2):
        cols = slice(512 * k, 512 * k + 512)
        h1_ref[:, cols] = (
            tok_ref[:, cols].astype(f32)
            + dot(gated, wo_ref[:, cols])
            + dot(mid_out, tb_ref[:, B_OUT + 512 * k : B_OUT + 512 * k + 512])
        )
    u2 = norm(h1_ref[...], n2_ref[...])[0].astype(bf16)
    u2_ref[...] = u2
    mg_ref[...] = (dot_nt(u2, tb_ref[:, A_GATE : A_GATE + D]).astype(bf16).astype(f32) * twice).astype(bf16)
    mu_ref[...] = (dot_nt(u2, tb_ref[:, A_UP : A_UP + D]).astype(bf16).astype(f32) * twice).astype(bf16)


def pre(seqs, length, count, *args):
    rows = seqs * length
    sd = jax.ShapeDtypeStruct
    width = D + 128
    vm = pl.BlockSpec(memory_space=pltpu.VMEM)
    wide = sd((rows, D), f32)
    half = sd((rows, D), bf16)
    thin = sd((rows, 128), bf16)
    return pl.pallas_call(
        functools.partial(pre_kernel, seqs, length, count),
        in_specs=[vm] * 10,
        out_specs=[vm] * 14,
        out_shape=[half, thin, wide, wide, wide, wide, sd((2, rows, 128), f32), half, thin, wide, half, thin, thin, thin],
        scratch_shapes=[
            pltpu.VMEM((seqs, length + 8, width), f32),
            pltpu.VMEM((2 * seqs, width), f32),
            pltpu.VMEM((2 * seqs, width), f32),
            pltpu.SemaphoreType.DMA,
            pltpu.SemaphoreType.DMA,
        ],
        compiler_params=pltpu.CompilerParams(vmem_limit_bytes=60 * MIB, collective_id=0, has_side_effects=True),
    )(*args)


def ffn_kernel(
    seqs, length,
    u_ref, cot_ref, mg_ref, mu_ref, gd_ref, mask_ref, h1_ref, wg_ref, wu_ref, wd_ref, bg_ref, bu_ref, ad_ref, ag_ref, au_ref, bd_ref,
    out_ref, gn_ref, dbg_ref, dbu_ref, dad_ref, dag_ref, dau_ref, dbd_ref,
    acc_ref, dmid_ref, gmg_ref, gmu_ref,
):
    j = pl.program_id(0)

    @pl.when(j == 0)
    def _():
        for ref in (acc_ref, gn_ref, dmid_ref, gmg_ref, gmu_ref):
            ref[...] = jnp.zeros_like(ref)

    u = u_ref[...]
    gate = dot(u, wg_ref[...]) + dot(mg_ref[...], bg_ref[...])
    up = dot(u, wu_ref[...]) + dot(mu_ref[...], bu_ref[...])
    back = dot_nt(cot_ref[...], wd_ref[...]) + dot(gd_ref[...], ad_ref[...])
    sig = jax.nn.sigmoid(gate)
    silu = gate * sig
    hidden = (silu * up).astype(bf16)
    grad_gate = (back * up * sig * (1.0 + gate * (1.0 - sig))).astype(bf16)
    grad_up = (back * silu).astype(bf16)
    acc_ref[...] += dot(hidden, wd_ref[...])
    gn_ref[...] += dot_nt(grad_gate, wg_ref[...]) + dot_nt(grad_up, wu_ref[...])
    dmid_ref[...] += dot_nt(hidden, ad_ref[...])
    gmg_ref[...] += dot_nt(grad_gate, bg_ref[...])
    gmu_ref[...] += dot_nt(grad_up, bu_ref[...])
    dbg_ref[...] = dot_tn(mg_ref[...], grad_gate).astype(bf16)
    dbu_ref[...] = dot_tn(mu_ref[...], grad_up).astype(bf16)
    dad_ref[...] = dot_tn(gd_ref[...], hidden).astype(bf16)

    @pl.when(j == pl.num_programs(0) - 1)
    def _():
        twice = 2.0 * row_mask(mask_ref, seqs, length)
        dmid = (dmid_ref[...].astype(bf16).astype(f32) * twice).astype(bf16)
        out_ref[...] = (h1_ref[...] + acc_ref[...] + dot(dmid, bd_ref[...])).astype(bf16)
        dbd_ref[...] = dot_tn(dmid, cot_ref[...]).astype(bf16)
        gm_gate = (gmg_ref[...] * twice).astype(bf16)
        gm_up = (gmu_ref[...] * twice).astype(bf16)
        gn_ref[...] += dot(gm_gate, ag_ref[...]) + dot(gm_up, au_ref[...])
        dag_ref[...] = dot_tn(gm_gate, u_ref[...]).astype(bf16)
        dau_ref[...] = dot_tn(gm_up, u_ref[...]).astype(bf16)


def ffn(seqs, length, u2, cot, mg, mu, gd, mask, h1, wg, wu, wd, table):
    rows = seqs * length
    sd = jax.ShapeDtypeStruct
    whole = lambda s: pl.BlockSpec(s, lambda j: (0, 0))
    col = lambda h: pl.BlockSpec((h, FB), lambda j: (0, j))
    tab = lambda first: pl.BlockSpec((128, FB), lambda j: (0, first // FB + j))
    fixed = lambda first: pl.BlockSpec((128, D), lambda j: (0, 0))
    cut = lambda first: lax.slice_in_dim(table, first, first + D, axis=1)
    return pl.pallas_call(
        functools.partial(ffn_kernel, seqs, length),
        grid=(FF // FB,),
        in_specs=[whole((rows, D)), whole((rows, D)), whole((rows, 128)), whole((rows, 128)), whole((rows, 128)),
                  whole(mask.shape), whole((rows, D)),
                  col(D), col(D), pl.BlockSpec((FB, D), lambda j: (j, 0)),
                  tab(B_GATE), tab(B_UP), tab(A_DOWN), whole((128, D)), whole((128, D)), whole((128, D))],
        out_specs=[whole((rows, D)), whole((rows, D)), col(128), col(128), col(128),
                   whole((128, D)), whole((128, D)), whole((128, D))],
        out_shape=[sd((rows, D), bf16), sd((rows, D), f32)] + [sd((128, FF), bf16)] * 3 + [sd((128, D), bf16)] * 3,
        scratch_shapes=[pltpu.VMEM((rows, D), f32)] + [pltpu.VMEM((rows, 128), f32)] * 3,
        compiler_params=pltpu.CompilerParams(vmem_limit_bytes=60 * MIB),
    )(u2, cot, mg, mu, gd, mask, h1, wg, wu, wd, table, table, table, cut(A_GATE), cut(A_UP), cut(B_DOWN))


def post_kernel(
    seqs, length, count,
    tok_ref, cot_ref, mask_ref, h1_ref, gn_ref, gated_ref, mo_ref, b_ref, c_ref, x_ref, conv_ref, same_ref, u1_ref, mi_ref,
    tb_ref, wi_ref, cw_ref, wo_ref, n1_ref, n2_ref,
    ig_ref, dai_ref, dbi_ref, dao_ref, dbo_ref,
    gh_ref, gb_ref, gg_ref, gc_ref, gp_ref, one_ref, two_ref, out_ref, in_ref, send_sem, recv_sem,
):
    seq = lax.axis_index("seq")
    greet(seq, count)
    twice = 2.0 * row_mask(mask_ref, seqs, length)
    h1 = h1_ref[...]
    inv2 = norm(h1, n2_ref[...])[1]
    e2 = gn_ref[...] * n2_ref[...]
    gh = cot_ref[...].astype(f32) + inv2 * e2 - h1 * (inv2 * inv2 * inv2 * jnp.mean(h1 * e2, axis=-1, keepdims=True))
    gh_ref[...] = gh
    gb = gh.astype(bf16)
    gb_ref[...] = gb
    gm_out = (dot_nt(gb, tb_ref[:, B_OUT : B_OUT + D]) * twice).astype(bf16)
    for k in range(2):
        cols = slice(512 * k, 512 * k + 512)
        gg_ref[:, cols] = dot_nt(gb, wo_ref[cols, :]) + dot(gm_out, tb_ref[:, A_OUT + 512 * k : A_OUT + 512 * k + 512])
    for s in range(seqs):
        rows = pl.ds(s * length, length)
        gg = gg_ref[rows, :]
        gp_ref[rows, D : 2 * D] = (gg * conv_ref[rows, :]).astype(bf16)
        gconv = gg * c_ref[rows, :]
        gc_ref[rows, :] = gconv
        one_ref[s, 0:length, :] = cw_ref[1:2, :] * same_ref[0, rows, 0:1] * gconv
        two_ref[s, 0:length, :] = cw_ref[0:1, :] * same_ref[1, rows, 0:1] * gconv
        one_ref[s, length:, :] = jnp.zeros((8, D), f32)
        two_ref[s, length:, :] = jnp.zeros((8, D), f32)
        out_ref[2 * s : 2 * s + 1, :] = two_ref[s, 0:1, :]
        out_ref[2 * s + 1 : 2 * s + 2, :] = two_ref[s, 1:2, :] + one_ref[s, 0:1, :]
    along = pltpu.make_async_remote_copy(
        src_ref=out_ref, dst_ref=in_ref, send_sem=send_sem, recv_sem=recv_sem,
        device_id={"seq": seq - 1}, device_id_type=MESH,
    )

    @pl.when(seq > 0)
    def _():
        along.start()

    dbo_ref[...] = dot_tn(mo_ref[...], gb).astype(bf16)
    dao_ref[...] = dot_tn(gm_out, gated_ref[...]).astype(bf16)

    @pl.when(seq > 0)
    def _():
        along.wait_send()

    @pl.when(seq < count - 1)
    def _():
        along.wait_recv()
        for s in range(seqs):
            two_ref[s, length : length + 2, :] = in_ref[2 * s : 2 * s + 2, :]

    for s in range(seqs):
        rows = pl.ds(s * length, length)
        gmix = (
            cw_ref[2:3, :] * gc_ref[rows, :]
            + one_ref[s, pl.ds(1, length), :]
            + two_ref[s, pl.ds(2, length), :]
        )
        gp_ref[rows, 0:D] = (gmix * x_ref[rows, :]).astype(bf16)
        gp_ref[rows, 2 * D :] = (gmix * b_ref[rows, :]).astype(bf16)
    gm_in = (dot_nt(gp_ref[...], tb_ref[:, B_IN : B_IN + 3 * D]) * twice).astype(bf16)
    for k in range(2):
        cols = slice(512 * k, 512 * k + 512)
        gg_ref[:, cols] = dot_nt(gp_ref[...], wi_ref[cols, :]) + dot(gm_in, tb_ref[:, A_IN + 512 * k : A_IN + 512 * k + 512])
    for k in range(6):
        cols = slice(512 * k, 512 * k + 512)
        dbi_ref[:, cols] = dot_tn(mi_ref[...], gp_ref[:, cols]).astype(bf16)
    dai_ref[...] = dot_tn(gm_in, u1_ref[...]).astype(bf16)
    tokens = tok_ref[...].astype(f32)
    inv1 = norm(tokens, n1_ref[...])[1]
    e1 = gg_ref[...] * n1_ref[...]
    ig_ref[...] = (
        gh_ref[...] + inv1 * e1 - tokens * (inv1 * inv1 * inv1 * jnp.mean(tokens * e1, axis=-1, keepdims=True))
    ).astype(bf16)


def post(seqs, length, count, *args):
    rows = seqs * length
    sd = jax.ShapeDtypeStruct
    vm = pl.BlockSpec(memory_space=pltpu.VMEM)
    return pl.pallas_call(
        functools.partial(post_kernel, seqs, length, count),
        in_specs=[vm] * 20,
        out_specs=[vm] * 5,
        out_shape=[sd((rows, D), bf16), sd((128, D), bf16), sd((128, 3 * D), bf16), sd((128, D), bf16), sd((128, D), bf16)],
        scratch_shapes=[
            pltpu.VMEM((rows, D), f32),
            pltpu.VMEM((rows, D), bf16),
            pltpu.VMEM((rows, D), f32),
            pltpu.VMEM((rows, D), f32),
            pltpu.VMEM((rows, 3 * D), bf16),
            pltpu.VMEM((seqs, length + 8, D), f32),
            pltpu.VMEM((seqs, length + 8, D), f32),
            pltpu.VMEM((2 * seqs, D), f32),
            pltpu.VMEM((2 * seqs, D), f32),
            pltpu.SemaphoreType.DMA,
            pltpu.SemaphoreType.DMA,
        ],
        compiler_params=pltpu.CompilerParams(vmem_limit_bytes=62 * MIB, collective_id=1, has_side_effects=True),
    )(*args)


def per_device(
    tokens, segment_ids, adapter_ids, input_weight, conv_weight, output_weight, gate_weight, up_weight, down_weight,
    norm_one, norm_two, cotangent, adapter_state, first_moment, second_moment, rate, step,
):
    seqs, length, _ = tokens.shape
    na = adapter_state.shape[0]
    groups = lax.axis_size("grp")
    count = lax.axis_size("seq")
    native = lambda x: x.reshape(na, PACKROWS, 128).swapaxes(0, 1).reshape(na * PACKROWS, 128)
    st, m, v = native(adapter_state), native(first_moment), native(second_moment)
    own = build_table(st, na)
    table = lax.all_gather(own, "grp", axis=0, tiled=True)
    adapters = na * groups
    mask = (adapter_ids[:, None] == jnp.arange(adapters * RANK, dtype=jnp.int32)[None, :] // RANK).astype(f32)
    ids = segment_ids.astype(f32)
    rows = seqs * length
    tok2, cot2 = tokens.reshape(rows, D), cotangent.reshape(rows, D)
    n1, n2 = norm_one.reshape(1, D), norm_two.reshape(1, D)
    u1, mi, b, c, x, conv, same, gated, mo, h1, u2, mg, mu, gd = pre(
        seqs, length, count, tok2, ids, mask, table, input_weight, conv_weight, output_weight, n1, n2, cot2
    )
    out, gn, dbg, dbu, dad, dag, dau, dbd = ffn(
        seqs, length, u2, cot2, mg, mu, gd, mask, h1, gate_weight, up_weight, down_weight, table
    )
    ig, dai, dbi, dao, dbo = post(
        seqs, length, count, tok2, cot2, mask, h1, gn, gated, mo, b, c, x, conv, same, u1, mi,
        table, input_weight, conv_weight, output_weight, n1, n2,
    )
    grads = jnp.concatenate([dai, dbi, dao, dbo, dag, dbg, dau, dbu, dad, dbd], axis=1).astype(f32)
    owned = lax.psum(lax.psum_scatter(grads, "grp", scatter_dimension=0, tiled=True), "seq")
    correction = 1.0 - jnp.power(jnp.float32(0.5), step[0].astype(f32))
    scal = jnp.stack([rate[0], 1.0 / correction])
    new, tab = adam(scal, owned, st, m, v, na)
    every = lax.all_gather(tab, "grp", axis=0, tiled=False)
    every = every.reshape(groups, PACKROWS, na, 128).transpose(0, 2, 1, 3).reshape(adapters, PACKROWS * 128)
    new = new.reshape(PACKROWS, na, 128).swapaxes(0, 1).reshape(na, PACKROWS * 128)
    return out.reshape(tokens.shape), ig.reshape(tokens.shape), new, every


def solution(mesh):
    rows = P("grp", "seq", None)
    own = P("grp", None)
    return jax.shard_map(
        per_device,
        mesh=mesh,
        in_specs=(rows, P("grp", "seq"), P("grp")) + (P(),) * 8 + (rows, own, own, own, P(), P()),
        out_specs=(rows, rows, own, P()),
        check_vma=False,
    )
```

time: 716 us -> 471 us (0.66)
  matrix products: 160 us -> 0 us
  Pallas kernels: 0 us -> 110 us
  local copies, waits for them, and re-layouts: 105 us -> 30.8 us
  waiting for transfers between devices: 373 us -> 306 us
  other arithmetic: 45.6 us -> 7.38 us
  starting transfers between devices: 11.1 us -> 0.42 us
    unnamed x5 -> x4, waiting for transfers between devices: 207 us -> 0.07 us
    dot_general x41 -> x0, matrix products: 160 us -> none  [the longest x5 35.2 us: dense_product(): jnp.einsum('spk,kn->spn', input_rows, weight_matrix, preferred_element_ty...]
    pallas_call x0 -> x5, Pallas kernels: none -> 110 us  [the longest x1 50.4 us: ffn(): pl.pallas_call(functools.partial(ffn_kernel, seqs, length), grid=(FF // F...]
    reduce_scatter x0 -> x1, waiting for transfers between devices: none -> 92.2 us  [per_device(): lax.psum_scatter(grads, 'grp', scatter_dimension=0, tiled=True)]
    all_gather x2, waiting for transfers between devices: 43.4 us -> 89 us  [the longest x1 45.7 us: per_device(): table = lax.all_gather(own, 'grp', axis=0, tiled=True)]
    reshape x10 -> x0, local copies, waits for them, and re-layouts: 36.2 us -> none  [the longest x5 21.6 us: per_device(): tensor_part.reshape(tensor_part.shape[0], -1)]
    gather x4 -> x0, local copies, waits for them, and re-layouts: 20.3 us -> none  [per_device(): pieces_list = unpack(jnp.take(table, adapter_ids, axis=0))]
    unnamed x174 -> x31, local copies, waits for them, and re-layouts: 42.1 us -> 25.4 us
  transfers between devices with their start and end apart: 7 -> 4, of which waited for: 4 -> 4; matrix products, arithmetic and copies ran while one was open for 14% -> 0% of each run, Pallas kernels for 0% -> 0%
where the time goes in v1:
time: 471 us; the launch traced here: 470 us
  waiting for transfers between devices  306 us (65%)
  Pallas kernels  110 us (23%)
  local copies, waits for them, and re-layouts  30.8 us (7%)
  between operations  15.4 us (3%)
  other arithmetic  7.38 us (2%)
    psum x1, waiting for transfers between devices, per_device(): lax.psum(lax.psum_scatter(grads, 'grp', scatter_dimension=0, tiled=True),...  125 us
    reduce_scatter x1, waiting for transfers between devices, per_device(): lax.psum_scatter(grads, 'grp', scatter_dimension=0, tiled=True)  92.2 us
    pallas_call x1, Pallas kernels, ffn(): pl.pallas_call(functools.partial(ffn_kernel, seqs, length), grid=(FF // F...  50.4 us
    all_gather x1, waiting for transfers between devices, per_device(): table = lax.all_gather(own, 'grp', axis=0, tiled=True)  45.7 us
    all_gather x1, waiting for transfers between devices, per_device(): every = lax.all_gather(tab, 'grp', axis=0, tiled=False)  43.3 us
    pallas_call x1, Pallas kernels, post(): pl.pallas_call(functools.partial(post_kernel, seqs, length, count), in_sp...  27.6 us
    unnamed x31, local copies, waits for them, and re-layouts  25.4 us
    pallas_call x1, Pallas kernels, pre(): pl.pallas_call(functools.partial(pre_kernel, seqs, length, count), in_spe...  19.2 us
  transfers between devices with their start and end apart: 4, of which 4 were waited for; matrix products, arithmetic and copies ran while one was open for 0% of the time, Pallas kernels for 0%

profile of v1, /device:TPU:0, one launch (start us, length us, event | category | flops | bytes accessed | tf_op | source)
XLA Modules:
  0.0 470.5 jit_solution(10486174662809651224)
XLA Ops:
  7.2 0.0 all-gather.4.cloned.1.call-start
  7.2 1.8 copy-done
  9.1 2.5 shard_map.192
  11.6 0.0 all-gather.4.cloned.1.call-update
  11.6 0.0 reduce-scatter.2.cloned.1.call-start
  11.7 0.6 convert_element_type.13.ids_ref
  12.3 0.7 compare_convert_fusion.mask_ref
  12.9 45.7 %all-gather.4.cloned.1.call-done.tb_ref.bg_ref.bu_ref.ad_ref = bf16[128,23040]{1,0:T(8,128)(2,1)} async-done(((bf16[32,23040]{1,0:T(8,128)(2,1)}), bf16[128,23040]{1,0:T(8,128)(2,1)}) %all-gather.4.cloned.1.call-update) | async-done | bytes 5898256 | tf_op jit(solution)/shard_map/all_gather | solution.py:447
  58.6 2.0 fusion
  60.6 19.2 %shard_map.193 = (bf16[512,1024]{1,0:T(8,128)(2,1)}, bf16[512,128]{1,0:T(8,128)(2,1)}, f32[512,1024]{1,0:T(8,128)}, f32[512,1024]{1,0:T(8,128)}, f32[512,1024]{1...) custom-call(bf16[512,1024]{1,0:T(8,128)(2,1)} %bitcast.42, ...), custom_call_target="tpu_custom_call" | custom-call | tf_op jit(solution)/shard_map/pallas_call | solution.py:247
  79.9 50.4 %shard_map.194 = (bf16[512,1024]{1,0:T(8,128)(2,1)}, f32[512,1024]{1,0:T(8,128)}, bf16[128,4608]{1,0:T(8,128)(2,1)}, bf16[128,4608]{1,0:T(8,128)(2,1)}, bf16[128...) custom-call(bf16[512,1024]{1,0:T(8,128)(2,1)} %get-tuple-element.33.u_ref,, ...), custom_call_target="tpu_custom_call" | custom-call | tf_op jit(solution)/shard_map/pallas_call | solution.py:315
  130.3 27.6 %shard_map.195 = (bf16[512,1024]{1,0:T(8,128)(2,1)}, bf16[128,1024]{1,0:T(8,128)(2,1)}, bf16[128,3072]{1,0:T(8,128)(2,1)}, bf16[128,1024]{1,0:T(8,128)(2,1)}, bf16[128,1024]{1,0:T(8,128)(2,1)}) custom-call(bf16[512,1024]{1,0:T(8,128)(2,1)} %bitcast.43, bf16[512,1024]{1,0:T(8,128)(2,1)} %bitcast.39, f32[4,128]{1,0:T(4,128)} %compare_convert_fusion.mask_ref, ...), custom_call_target="tpu_custom_call" | custom-call | tf_op jit(solution)/shard_map/pallas_call | solution.py:414
  157.9 1.1 constant_dynamic-update-slice_fusion.9
  159.1 1.2 constant_dynamic-update-slice_fusion.8
  160.3 1.0 constant_dynamic-update-slice_fusion.7
  161.2 1.0 constant_dynamic-update-slice_fusion.6
  162.2 0.1 constant_dynamic-update-slice_fusion.4
  162.4 0.1 constant_dynamic-update-slice_fusion.2
  162.5 0.1 constant_dynamic-update-slice_fusion.1
  162.6 5.5 %convert_element_type.16 = f32[128,23040]{1,0:T(8,128)} convert(bf16[128,23040]{1,0:T(8,128)(2,1)S(1)} %constant_dynamic-update-slice_fusion) | non-fusion elementwise | flops 2949120 | bytes 17694720 | tf_op jit(solution)/shard_map/convert_element_type | solution.py:464
  168.2 0.0 all-reduce.2.cloned.1.call-start
  168.2 92.2 %reduce-scatter.2.cloned.1.call-done = f32[32,23040]{1,0:T(8,128)} async-done(((f32[128,23040]{1,0:T(8,128)}), f32[32,23040]{1,0:T(8,128)}) %reduce-scatter.2.cloned.1.call-update) | async-done | bytes 2949136 | tf_op jit(solution)/shard_map/reduce_scatter | solution.py:465
  260.4 0.0 all-reduce.2.cloned.1.call-update
  260.4 0.3 all-gather.6.cloned.1.call-start
  262.1 0.6 pad_maximum_fusion.scal_ref
  262.7 124.9 %all-reduce.2.cloned.1.call-done.gw_ref = f32[32,23040]{1,0:T(8,128)} async-done(((f32[32,23040]{1,0:T(8,128)}), f32[32,23040]{1,0:T(8,128)}) %all-reduce.2.cloned.1.call-update) | async-done | bytes 2949136 | tf_op jit(solution)/shard_map/psum | solution.py:465
  387.6 10.6 %shard_map.196 = (f32[5760,128]{1,0:T(8,128)}, bf16[5760,128]{1,0:T(8,128)(2,1)}) custom-call(f32[2]{0:T(128)} %pad_maximum_fusion.scal_ref, f32[32,23040]{1,0:T(8,128)} %all-reduce.2.cloned.1.call-done.gw_ref, f32[5760,128]{1,0:T(8,128)} %bitcast.34, f32[5760,128]{1,0:T(8,128)} %bitcast.44, f32[5760,128]{1,0:T(8,128)} %bitcast.45), custom_call_target="tpu_custom_call" | custom-call | tf_op jit(solution)/shard_map/pallas_call | solution.py:116
  398.2 0.0 all-gather.6.cloned.1.call-update
  398.2 43.3 %all-gather.6.cloned.1.call-done = bf16[23040,128]{1,0:T(8,128)(2,1)} async-done(((bf16[5760,128]{1,0:T(8,128)(2,1)}), bf16[23040,128]{1,0:T(8,128)(2,1)}) %all-gather.6.cloned.1.call-update) | async-done | bytes 5898256 | tf_op jit(solution)/shard_map/all_gather | solution.py:469
  441.5 3.4 copy.25
  445.0 18.0 %copy.28 = bf16[1,8,2880,128]{3,1,2,0:T(8,128)(2,1)} copy(bf16[1,8,2880,128]{3,2,1,0:T(8,128)(2,1)S(1)} %bitcast.36) | data formatting | bytes 11796480
  463.0 1.0 copy.42
  (24 shorter events, 0.1 us)
Async XLA Ops:
  7.2 5.1 %copy-start.9 = (s32[4]{0:T(128)S(1)}, s32[4]{0:T(128)}, u32[]{:S(2)}) copy-start(s32[4]{0:T(128)} %param.19) | copy-start | bytes 52
  7.2 51.5 %all-gather.4.cloned.1.call-start = ((), (), s32[]{:S(2)}) async-start(), calls=%async_computation.1 | async-start | bytes 7372800 | tf_op jit(solution)/shard_map/all_gather | solution.py:447
  7.2 1.8 copy-start
  9.1 2.6 copy-start.8
  11.6 248.8 %reduce-scatter.2.cloned.1.call-start = ((), (), s32[]{:S(2)}) async-start(), calls=%async_computation.2 | async-start | bytes 14745600 | tf_op jit(solution)/shard_map/reduce_scatter | solution.py:465
  130.3 31.9 %copy-start.7 = (bf16[128,1024]{1,0:T(8,128)(2,1)S(1)}, bf16[128,1024]{1,0:T(8,128)(2,1)}, u32[]{:S(2)}) copy-start(bf16[128,1024]{1,0:T(8,128)(2,1)} %get-tuple-element.54) | copy-start | bytes 786436
  130.3 31.9 %copy-start.3 = (bf16[128,4608]{1,0:T(8,128)(2,1)S(1)}, bf16[128,4608]{1,0:T(8,128)(2,1)}, u32[]{:S(2)}) copy-start(bf16[128,4608]{1,0:T(8,128)(2,1)} %get-tuple-element.55) | copy-start | bytes 3538948
  157.9 4.4 copy-start.6
  157.9 4.5 copy-start.2
  157.9 4.5 copy-start.1
  157.9 4.6 copy-start.5
  168.2 219.4 %all-reduce.2.cloned.1.call-start = ((), (), s32[]{:S(2)}) async-start(), calls=%async_computation.3 | async-start | bytes 5898240 | tf_op jit(solution)/shard_map/psum | solution.py:465
  260.4 181.1 %all-gather.6.cloned.1.call-start = ((), (), s32[]{:S(2)}) async-start(), calls=%async_computation.4 | async-start | bytes 7372800 | tf_op jit(solution)/shard_map/all_gather | solution.py:469
  445.0 18.0 %copy-start.4 = (bf16[512,1024]{1,0:T(8,128)(2,1)S(1)}, bf16[512,1024]{1,0:T(8,128)(2,1)}, u32[]{:S(2)}) copy-start(bf16[512,1024]{1,0:T(8,128)(2,1)} %get-tuple-element.49) | copy-start | bytes 3145732
Sparse Core Ops, SparseCore 0:
  11.8 46.8 all-gather.3
  168.3 92.0 reduce-scatter.1
  264.0 123.4 all-reduce.1
  398.3 43.1 all-gather.5

commit v2 on v1

--- a/solution.py
+++ b/solution.py
@@ -433,7 +433,7 @@
     )(*args)
 
 
-def per_device(
+def general_device(
     tokens, segment_ids, adapter_ids, input_weight, conv_weight, output_weight, gate_weight, up_weight, down_weight,
     norm_one, norm_two, cotangent, adapter_state, first_moment, second_moment, rate, step,
 ):
@@ -467,7 +467,1008 @@
     scal = jnp.stack([rate[0], 1.0 / correction])
     new, tab = adam(scal, owned, st, m, v, na)
     every = lax.all_gather(tab, "grp", axis=0, tiled=False)
-    every = every.reshape(groups, PACKROWS, na, 128).transpose(0, 2, 1, 3).reshape(adapters, PACKROWS * 128)
+    every = every.reshape(groups, PACKROWS, na, 128).transpose(1, 0, 2, 3).reshape(PACKROWS, adapters, 128)
+    every = every.swapaxes(0, 1).reshape(adapters, PACKROWS * 128)
+    new = new.reshape(PACKROWS, na, 128).swapaxes(0, 1).reshape(na, PACKROWS * 128)
+    return out.reshape(tokens.shape), ig.reshape(tokens.shape), new, every
+
+
+W_A_IN, W_B_B, W_B_X, W_B_C, W_A_OUT, W_B_OUT, W_A_GATE, W_A_UP, W_B_DOWN, W_FFN = (1024 * n for n in range(10))
+W_ENDS = W_A_GATE
+BLOCKS = FF // FB
+W_BLOCK = 3 * FB
+FFN_COLS = WIRE - W_ENDS
+SPREAD_BLOCKS = 2
+
+
+def wire(first, n):
+    if first == B_IN:
+        return (W_B_B, W_B_C, W_B_X)[n // D] + n % D
+    for place, matrix in enumerate((B_GATE, B_UP, A_DOWN)):
+        if first == matrix:
+            return W_FFN + n // FB * W_BLOCK + place * FB + n % FB
+    return {A_IN: W_A_IN, A_OUT: W_A_OUT, B_OUT: W_B_OUT, A_GATE: W_A_GATE, A_UP: W_A_UP, B_DOWN: W_B_DOWN}[first] + n
+
+
+def a_pieces(first, count):
+    for matrix, height in A_PARTS:
+        if matrix <= first < matrix + height:
+            return [(k, wire(matrix, first - matrix + k), FB) for k in range(0, count, FB)]
+
+
+class Place:
+    def __init__(self):
+        seq, grp = lax.axis_index("seq"), lax.axis_index("grp")
+        self.seq, self.grp = seq, grp
+        self.c, self.x, self.y, self.z = grp % 2, grp // 2, seq % 2, seq // 2
+        self.core = grp + 1 - 2 * self.c
+        self.gx = (grp + 2) % 4
+        self.sy = seq + 1 - 2 * self.y
+        self.sz = seq + 2 - 4 * (self.z % 2)
+
+    def along_z(self, d):
+        return (self.seq + 2 * d) % 8
+
+
+def announce(seq, count, devices, both=True):
+    barrier = pltpu.get_barrier_semaphore()
+    if both:
+
+        @pl.when(seq > 0)
+        def _():
+            pl.semaphore_signal(barrier, inc=1, device_id={"seq": seq - 1}, device_id_type=MESH)
+
+        @pl.when(seq < count - 1)
+        def _():
+            pl.semaphore_signal(barrier, inc=1, device_id={"seq": seq + 1}, device_id_type=MESH)
+
+    for device in devices:
+        pl.semaphore_signal(barrier, inc=1, device_id=device, device_id_type=MESH)
+    ends = (seq + count - 1) // count + (2 * count - 2 - seq) // count if both else 0
+    return lambda: pl.semaphore_wait(barrier, ends + len(devices))
+
+
+class Spread:
+    KINDS = ("core", "x", "y", "z", "dy", "dz", "cx", "cy", "cz", "cd")
+
+    def __init__(self, at, own, slot, pieces, step, send_sems, recv_sems):
+        self.at, self.own, self.slot, self.pieces, self.step = at, own, slot, pieces, step
+        self.send_sems, self.recv_sems = send_sems, recv_sems
+
+    def copy(self, kind, p):
+        at = self.at
+        first, size = self.pieces[p]
+        quarter = size // 4
+        half = -(-quarter // (2 * self.step)) * self.step
+        part = lambda q: pl.multiple_of(first + q * quarter, self.step)
+        q = at.seq % 4
+        qy, qz, qd = q + 1 - 2 * (q % 2), (q + 2) % 4, 3 - q
+        core, y, z = {"grp": at.core}, {"seq": at.sy}, {"seq": at.sz}
+        if kind == "core":
+            src, dst, device = self.own(first, size), self.slot(at.grp, first, size), core
+        elif kind == "x":
+            src, dst, device = self.own(part(q), quarter), self.slot(at.grp, part(q), quarter), {"grp": at.gx}
+        else:
+            start, count, device = {
+                "y": (part(q), quarter, y),
+                "z": (part(q), quarter, z),
+                "dy": (part(qz), half, y),
+                "dz": (pl.multiple_of(part(qy) + half, self.step), quarter - half, z),
+                "cx": (part(q), quarter, core),
+                "cy": (part(qy), quarter, core),
+                "cz": (part(qz), quarter, core),
+                "cd": (part(qd), quarter, core),
+            }[kind]
+            src = dst = self.slot(at.gx, start, count)
+        n = len(self.KINDS) * p + self.KINDS.index(kind)
+        return pltpu.make_async_remote_copy(
+            src_ref=src, dst_ref=dst, send_sem=self.send_sems.at[n], recv_sem=self.recv_sems.at[n],
+            device_id=device, device_id_type=MESH,
+        )
+
+    def leg(self, number, p):
+        waits, starts = (
+            ((), ("x", "core")),
+            (("x",), ("y", "z", "cx")),
+            (("y",), ("dz", "cy")),
+            (("z",), ("dy", "cz")),
+            (("dy", "dz"), ("cd",)),
+            (("core", "cx", "cy", "cz", "cd"), ()),
+        )[number]
+        for kind in waits:
+            self.copy(kind, p).wait_recv()
+        for kind in starts:
+            self.copy(kind, p).start()
+
+    def sent(self, p):
+        for kind in self.KINDS:
+            self.copy(kind, p).wait_send()
+
+
+def fill_shuffle(perm_ref):
+    diff = lax.broadcasted_iota(jnp.int32, (128, 1024), 1) - 8 * lax.broadcasted_iota(jnp.int32, (128, 1024), 0)
+    for c in range(8):
+        perm_ref[128 * c : 128 * c + 128, :] = jnp.where(diff == c, 1.0, 0.0).astype(bf16)
+
+
+def build_own(na, grp, st_ref, tb_ref, lhs_ref, perm_ref):
+    own = lambda a: pl.ds(pl.multiple_of((grp * na + a) * RANK, RANK), RANK)
+    fill_shuffle(perm_ref)
+    for n, (first, count) in enumerate(A_CHUNKS):
+        for a in range(na):
+            packed = st_ref[pl.ds(na * (first // 8) + a, 128, stride=na), :]
+            turned = packed.T.astype(bf16)
+            row = (n * na + a) * RANK
+            for c in range(8):
+                lhs_ref[row : row + RANK, 128 * c : 128 * c + 128] = turned[RANK * c : RANK * c + RANK, :]
+    full = dot(lhs_ref[...], perm_ref[...]).astype(bf16)
+    for n, (first, count) in enumerate(A_CHUNKS):
+        for a in range(na):
+            row = (n * na + a) * RANK
+            for k, col, size in a_pieces(first, count):
+                tb_ref[own(a), col : col + size] = full[row : row + RANK, k : k + size]
+    for first, breadth in B_PARTS:
+        blocks = breadth // 128
+        for a in range(na):
+            for c in range(blocks):
+                part = st_ref[pl.ds(na * (first // 8 + c) + a, RANK, stride=na * blocks), :]
+                col = wire(first, 128 * c)
+                tb_ref[own(a), col : col + 128] = part.astype(bf16)
+
+
+SPREAD_PIECES = ((0, 4096), (W_A_OUT, 5120), (W_FFN, SPREAD_BLOCKS * W_BLOCK))
+
+
+def start_kernel(
+    seqs, length, count, na,
+    st_ref, tok_ref, ids_ref, mask_ref, wi_hbm, cw_ref, wo_hbm, n1_ref, n2_ref,
+    tb_hbm, u1_hbm, mi_ref, b_hbm, c_hbm, x_hbm, conv_hbm, same_hbm, gated_hbm, mo_ref, h1_hbm, u2_hbm, mg_ref, mu_ref,
+    tb_ref, lhs_ref, perm_ref, wi_ref, wo_ref, u1_ref, b_ref, c_ref, x_ref, conv_ref, same_ref, gated_ref, h1_ref, u2_ref,
+    ext_ref, out_ref, in_ref, halo_sems, load_sems, store_sems, send_sems, recv_sems,
+):
+    at = Place()
+    seq, grp = at.seq, at.grp
+    load_in = pltpu.make_async_copy(wi_hbm, wi_ref, load_sems.at[0])
+    load_out = pltpu.make_async_copy(wo_hbm, wo_ref, load_sems.at[1])
+    load_in.start()
+    load_out.start()
+    met = announce(seq, count, ({"grp": at.core}, {"grp": at.gx}, {"seq": at.sz}))
+    build_own(na, grp, st_ref, tb_ref, lhs_ref, perm_ref)
+    height = na * RANK
+    block = lambda owner, first, size: tb_ref.at[
+        pl.ds(pl.multiple_of(owner * height, height), height), pl.ds(first, size)
+    ]
+    spread = Spread(at, functools.partial(block, grp), block, SPREAD_PIECES, 128, send_sems, recv_sems)
+    leg = spread.leg
+
+    def keep(n, src, dst):
+        return pltpu.make_async_copy(src, dst, store_sems.at[n])
+
+    met()
+    leg(0, 0)
+    twice = 2.0 * row_mask(mask_ref, seqs, length)
+    tokens = tok_ref[...].astype(f32)
+    u1 = norm(tokens, n1_ref[...])[0].astype(bf16)
+    u1_ref[...] = u1
+    keep(0, u1_ref, u1_hbm).start()
+    load_in.wait()
+    for k in range(2):
+        b_ref[:, 512 * k : 512 * k + 512] = dot(u1, wi_ref[:, 512 * k : 512 * k + 512])
+    leg(1, 0)
+    for p in range(1, len(SPREAD_PIECES)):
+        leg(0, p)
+    for k in range(2):
+        x_ref[:, 512 * k : 512 * k + 512] = dot(u1, wi_ref[:, 2 * D + 512 * k : 2 * D + 512 * k + 512])
+    leg(1, 1)
+    leg(2, 0)
+    leg(3, 0)
+    for k in range(2):
+        c_ref[:, 512 * k : 512 * k + 512] = dot(u1, wi_ref[:, D + 512 * k : D + 512 * k + 512])
+    leg(1, 2)
+    leg(4, 0)
+    leg(5, 0)
+    mid = (dot_nt(u1, tb_ref[:, W_A_IN : W_A_IN + D]).astype(bf16).astype(f32) * twice).astype(bf16)
+    mi_ref[...] = mid
+    for first, to_ref in ((W_B_B, b_ref), (W_B_X, x_ref)):
+        for k in range(2):
+            col = first + 512 * k
+            to_ref[:, 512 * k : 512 * k + 512] += dot(mid, tb_ref[:, col : col + 512])
+    leg(2, 1)
+    leg(3, 1)
+    keep(1, b_ref, b_hbm).start()
+    keep(2, x_ref, x_hbm).start()
+    width = D + 128
+    for s in range(seqs):
+        rows = pl.ds(s * length, length)
+        ext_ref[s, 0:8, :] = jnp.zeros((8, width), f32)
+        ext_ref[s, 8:, :D] = b_ref[rows, :] * x_ref[rows, :]
+        ext_ref[s, 8:, D:] = jnp.broadcast_to(ids_ref[s : s + 1, :], (length, 128)).T
+        out_ref[2 * s : 2 * s + 2, :] = ext_ref[s, length + 6 : length + 8, :]
+    along = pltpu.make_async_remote_copy(
+        src_ref=out_ref, dst_ref=in_ref, send_sem=halo_sems.at[0], recv_sem=halo_sems.at[1],
+        device_id={"seq": seq + 1}, device_id_type=MESH,
+    )
+
+    @pl.when(seq < count - 1)
+    def _():
+        along.start()
+
+    for k in range(2):
+        col = W_B_C + 512 * k
+        c_ref[:, 512 * k : 512 * k + 512] += dot(mid, tb_ref[:, col : col + 512])
+    keep(3, c_ref, c_hbm).start()
+    leg(2, 2)
+    leg(3, 2)
+
+    @pl.when(seq < count - 1)
+    def _():
+        along.wait_send()
+
+    @pl.when(seq > 0)
+    def _():
+        along.wait_recv()
+        for s in range(seqs):
+            ext_ref[s, 6:8, :] = in_ref[2 * s : 2 * s + 2, :]
+
+    for s in range(seqs):
+        rows = pl.ds(s * length, length)
+        now_ids = ext_ref[s, 8:, D:]
+        same1 = jnp.where(ext_ref[s, pl.ds(7, length), D:] == now_ids, 1.0, 0.0)
+        same2 = jnp.where(ext_ref[s, pl.ds(6, length), D:] == now_ids, 1.0, 0.0)
+        same_ref[0, rows, :] = same1
+        same_ref[1, rows, :] = same2
+        conv = (
+            cw_ref[2:3, :] * ext_ref[s, 8:, :D]
+            + cw_ref[1:2, :] * same1[:, :1] * ext_ref[s, pl.ds(7, length), :D]
+            + cw_ref[0:1, :] * same2[:, :1] * ext_ref[s, pl.ds(6, length), :D]
+        )
+        conv_ref[rows, :] = conv
+        gated_ref[rows, :] = (c_ref[rows, :] * conv).astype(bf16)
+    keep(4, conv_ref, conv_hbm).start()
+    keep(5, same_ref, same_hbm).start()
+    leg(4, 1)
+    leg(4, 2)
+    keep(6, gated_ref, gated_hbm).start()
+    gated = gated_ref[...]
+    load_out.wait()
+    for k in range(2):
+        cols = slice(512 * k, 512 * k + 512)
+        h1_ref[:, cols] = tok_ref[:, cols].astype(f32) + dot(gated, wo_ref[:, cols])
+    leg(5, 1)
+    mid_out = (dot_nt(gated, tb_ref[:, W_A_OUT : W_A_OUT + D]).astype(bf16).astype(f32) * twice).astype(bf16)
+    mo_ref[...] = mid_out
+    for k in range(2):
+        cols = slice(512 * k, 512 * k + 512)
+        h1_ref[:, cols] += dot(mid_out, tb_ref[:, W_B_OUT + 512 * k : W_B_OUT + 512 * k + 512])
+    keep(7, h1_ref, h1_hbm).start()
+    u2 = norm(h1_ref[...], n2_ref[...])[0].astype(bf16)
+    u2_ref[...] = u2
+    keep(8, u2_ref, u2_hbm).start()
+    keep(9, tb_ref.at[:, :W_FFN], tb_hbm.at[:, :W_FFN]).start()
+    mg_ref[...] = (dot_nt(u2, tb_ref[:, W_A_GATE : W_A_GATE + D]).astype(bf16).astype(f32) * twice).astype(bf16)
+    mu_ref[...] = (dot_nt(u2, tb_ref[:, W_A_UP : W_A_UP + D]).astype(bf16).astype(f32) * twice).astype(bf16)
+    leg(5, 2)
+    keep(10, tb_ref.at[:, W_FFN:], tb_hbm.at[:, W_FFN:]).start()
+    for p in range(len(SPREAD_PIECES)):
+        spread.sent(p)
+    for n, (src, dst) in enumerate((
+        (u1_ref, u1_hbm), (b_ref, b_hbm), (x_ref, x_hbm), (c_ref, c_hbm), (conv_ref, conv_hbm), (same_ref, same_hbm),
+        (gated_ref, gated_hbm), (h1_ref, h1_hbm), (u2_ref, u2_hbm),
+        (tb_ref.at[:, :W_FFN], tb_hbm.at[:, :W_FFN]), (tb_ref.at[:, W_FFN:], tb_hbm.at[:, W_FFN:]),
+    )):
+        keep(n, src, dst).wait()
+
+
+def start(seqs, length, count, na, *args):
+    rows = seqs * length
+    sd = jax.ShapeDtypeStruct
+    width = D + 128
+    vm = pl.BlockSpec(memory_space=pltpu.VMEM)
+    hbm = pl.BlockSpec(memory_space=pl.ANY)
+    table = sd((128, WIRE), bf16)
+    wide = sd((rows, D), f32)
+    half = sd((rows, D), bf16)
+    thin = sd((rows, 128), bf16)
+    same = sd((2, rows, 128), f32)
+    scratch = lambda x: pltpu.VMEM(x.shape, x.dtype)
+    return pl.pallas_call(
+        functools.partial(start_kernel, seqs, length, count, na),
+        in_specs=[vm, vm, vm, vm, hbm, vm, hbm, vm, vm],
+        out_specs=[hbm, hbm, vm, hbm, hbm, hbm, hbm, hbm, hbm, vm, hbm, hbm, vm, vm],
+        out_shape=[table, half, thin, wide, wide, wide, wide, same, half, thin, wide, half, thin, thin],
+        scratch_shapes=[
+            scratch(table),
+            pltpu.VMEM((len(A_CHUNKS) * na * RANK, 1024), bf16),
+            pltpu.VMEM((1024, 1024), bf16),
+            pltpu.VMEM((D, 3 * D), bf16),
+            pltpu.VMEM((D, D), bf16),
+            scratch(half), scratch(wide), scratch(wide), scratch(wide), scratch(wide), scratch(same), scratch(half),
+            scratch(wide), scratch(half),
+            pltpu.VMEM((seqs, length + 8, width), f32),
+            pltpu.VMEM((2 * seqs, width), f32),
+            pltpu.VMEM((2 * seqs, width), f32),
+            pltpu.SemaphoreType.DMA((2,)),
+            pltpu.SemaphoreType.DMA((2,)),
+            pltpu.SemaphoreType.DMA((11,)),
+            pltpu.SemaphoreType.DMA((len(Spread.KINDS) * len(SPREAD_PIECES),)),
+            pltpu.SemaphoreType.DMA((len(Spread.KINDS) * len(SPREAD_PIECES),)),
+        ],
+        compiler_params=pltpu.CompilerParams(vmem_limit_bytes=60 * MIB, collective_id=2, has_side_effects=True),
+    )(*args)
+
+
+class Sums:
+    CORE, X, Y, Z, BACK_Z, BACK_Y = range(6)
+    COPIES = 10
+
+    def __init__(self, at, g_ref, cr_ref, xr_ref, yr_ref, zr_ref, sum_ref, send_sems, recv_sems):
+        self.at, self.g, self.cr, self.xr, self.yr, self.zr, self.sum = at, g_ref, cr_ref, xr_ref, yr_ref, zr_ref, sum_ref
+        self.send_sems, self.recv_sems = send_sems, recv_sems
+
+    def unit(self, z, start, size):
+        rows = pl.ds(pl.multiple_of(RANK * (z // 2), RANK), RANK)
+        quarter = size // 4
+        return rows, pl.ds(pl.multiple_of(start + self.at.y * (size // 2) + (z % 2) * quarter, 128), quarter)
+
+    def half(self, y, start, size):
+        return pl.ds(pl.multiple_of(start + y * (size // 2), 128), size // 2)
+
+    def slot(self, start, size, share):
+        return pl.ds(pl.multiple_of(start // share, 128), size // share)
+
+    def copies(self, stage, group):
+        index, start, size = group
+        at = self.at
+        cols = pl.ds(start, size)
+        if stage == self.CORE:
+            parts = [(self.g.at[:, 1 - at.c, :, cols], self.cr.at[:, :, cols], {"grp": at.core})]
+        elif stage == self.X:
+            parts = [(self.g.at[1 - at.x, at.c, :, cols], self.xr.at[:, cols], {"grp": at.gx})]
+        elif stage == self.Y:
+            away = self.half(1 - at.y, start, size)
+            parts = [(self.g.at[at.x, at.c, :, away], self.yr.at[:, self.slot(start, size, 2)], {"seq": at.sy})]
+        elif stage == self.BACK_Y:
+            part = self.sum.at[:, self.half(at.y, start, size)]
+            parts = [(part, part, {"seq": at.sy})]
+        else:
+            parts = []
+            for d in range(1, 4):
+                if stage == self.Z:
+                    rows, span = self.unit((at.z + d) % 4, start, size)
+                    parts.append((
+                        self.g.at[at.x, at.c, rows, span], self.zr.at[d - 1, :, self.slot(start, size, 4)],
+                        {"seq": at.along_z(d)},
+                    ))
+                else:
+                    rows, span = self.unit(at.z, start, size)
+                    part = self.sum.at[rows, span]
+                    parts.append((part, part, {"seq": at.along_z(d)}))
+        first = self.COPIES * index + {self.CORE: 0, self.X: 1, self.Y: 2, self.Z: 3, self.BACK_Z: 6, self.BACK_Y: 9}[stage]
+        return [
+            pltpu.make_async_remote_copy(
+                src_ref=src, dst_ref=dst, send_sem=self.send_sems.at[first + n], recv_sem=self.recv_sems.at[first + n],
+                device_id=device, device_id_type=MESH,
+            )
+            for n, (src, dst, device) in enumerate(parts)
+        ]
+
+    def send(self, stage, group):
+        for copy in self.copies(stage, group):
+            copy.start()
+
+    def take(self, stage, group):
+        for copy in self.copies(stage, group):
+            copy.wait()
+        _, start, size = group
+        at = self.at
+        cols = pl.ds(start, size)
+        wide = lambda value: value.astype(f32)
+        if stage == self.CORE:
+            for x in range(2):
+                self.g[x, at.c, :, cols] = (wide(self.g[x, at.c, :, cols]) + wide(self.cr[x, :, cols])).astype(bf16)
+        elif stage == self.X:
+            self.g[at.x, at.c, :, cols] = (wide(self.g[at.x, at.c, :, cols]) + wide(self.xr[:, cols])).astype(bf16)
+        elif stage == self.Y:
+            mine = self.half(at.y, start, size)
+            came = self.yr[:, self.slot(start, size, 2)]
+            self.g[at.x, at.c, :, mine] = (wide(self.g[at.x, at.c, :, mine]) + wide(came)).astype(bf16)
+        elif stage == self.Z:
+            rows, span = self.unit(at.z, start, size)
+            total = wide(self.g[at.x, at.c, rows, span])
+            for d in range(3):
+                total = total + wide(self.zr[d, :, self.slot(start, size, 4)])
+            self.sum[rows, span] = total.astype(bf16)
+
+
+def sums_scratch(cols):
+    return [
+        pltpu.VMEM((2, 2, 32, cols), bf16),
+        pltpu.VMEM((2, 32, cols), bf16),
+        pltpu.VMEM((32, cols), bf16),
+        pltpu.VMEM((32, cols // 2), bf16),
+        pltpu.VMEM((3, 16, cols // 4), bf16),
+        pltpu.VMEM((32, cols), bf16),
+    ]
+
+
+def put_grad(g_ref, cols, value):
+    for x in range(2):
+        for c in range(2):
+            first = 64 * x + 32 * c
+            g_ref[x, c, :, cols] = value[first : first + 32, :].astype(bf16)
+
+
+ENDS_COLS = W_FFN - W_ENDS
+
+
+def ffn_group(j):
+    start = ENDS_COLS + j * W_BLOCK
+    return j, start if isinstance(j, int) else pl.multiple_of(start, 128), W_BLOCK
+
+
+def middle_kernel(
+    seqs, length,
+    u_ref, cot_ref, mg_ref, mu_ref, mask_ref, h1_hbm, wg_hbm, wu_hbm, wd_hbm, tb_hbm,
+    out_ref, gn_ref, g_hbm, sum_hbm,
+    tb_ref, wg_ref, wu_ref, wd_ref, h1_ref, acc_ref, dmid_ref, gmg_ref, gmu_ref, gd_ref,
+    g_ref, cr_ref, xr_ref, yr_ref, zr_ref, sum_ref,
+    load_sems, weight_sems, tab_send, tab_recv, send_sems, recv_sems,
+):
+    at = Place()
+    along = [{"seq": at.along_z(d)} for d in range(1, 4)]
+    met = announce(at.seq, 8, [{"grp": at.core}, {"grp": at.gx}, {"seq": at.sy}] + along, both=False)
+
+    def fetch(j, slot):
+        cols = pl.ds(j * FB if isinstance(j, int) else pl.multiple_of(j * FB, FB), FB)
+        return [
+            pltpu.make_async_copy(wg_hbm.at[:, cols], wg_ref.at[slot], weight_sems.at[slot, 0]),
+            pltpu.make_async_copy(wu_hbm.at[:, cols], wu_ref.at[slot], weight_sems.at[slot, 1]),
+            pltpu.make_async_copy(wd_hbm.at[cols, :], wd_ref.at[slot], weight_sems.at[slot, 2]),
+        ]
+
+    for copy in fetch(0, 0):
+        copy.start()
+    here = ENDS_COLS + SPREAD_BLOCKS * W_BLOCK
+    rows32 = lambda owner: pl.ds(pl.multiple_of(owner * 32, 32), 32)
+    loads = [
+        pltpu.make_async_copy(tb_hbm.at[:, W_ENDS : W_ENDS + here], tb_ref.at[:, :here], load_sems.at[0]),
+        pltpu.make_async_copy(
+            tb_hbm.at[rows32(at.grp), W_ENDS + here :], tb_ref.at[rows32(at.grp), here:], load_sems.at[1]
+        ),
+        pltpu.make_async_copy(h1_hbm, h1_ref, load_sems.at[2]),
+    ]
+    for copy in loads:
+        copy.start()
+
+    def table_copy(kind, j):
+        _, start, size = ffn_group(j)
+        owner, device = {
+            "core": (at.grp, {"grp": at.core}), "x": (at.grp, {"grp": at.gx}), "far": (at.gx, {"grp": at.core})
+        }[kind]
+        part = tb_ref.at[rows32(owner), pl.ds(start, size)]
+        n = 3 * j + ("core", "x", "far").index(kind)
+        return pltpu.make_async_remote_copy(
+            src_ref=part, dst_ref=part, send_sem=tab_send.at[n], recv_sem=tab_recv.at[n], device_id=device, device_id_type=MESH
+        )
+
+    sums = Sums(at, g_ref, cr_ref, xr_ref, yr_ref, zr_ref, sum_ref, send_sems, recv_sems)
+    twice = 2.0 * row_mask(mask_ref, seqs, length)
+    for ref in (acc_ref, gn_ref, dmid_ref, gmg_ref, gmu_ref):
+        ref[...] = jnp.zeros_like(ref)
+    loads[0].wait()
+    a_gate, a_up, b_down = (tb_ref.at[:, first - W_ENDS : first - W_ENDS + D] for first in (W_A_GATE, W_A_UP, W_B_DOWN))
+    gd_ref[...] = (dot_nt(cot_ref[...], b_down[...]) * twice).astype(bf16)
+    loads[1].wait()
+    met()
+
+    def when(first, j, last, run):
+        @pl.when((j >= first) & (j <= last))
+        def _():
+            run()
+
+    def block(j, carry):
+        slot = j % 2
+        for copy in fetch(j, slot):
+            copy.wait()
+
+        def more():
+            for copy in fetch(j + 1, 1 - slot):
+                copy.start()
+
+        when(0, j, BLOCKS - 2, more)
+        lead = SPREAD_BLOCKS
+
+        def leave():
+            table_copy("x", j + lead).start()
+            table_copy("core", j + lead).start()
+
+        def go_on():
+            table_copy("x", j + lead - 1).wait()
+            table_copy("far", j + lead - 1).start()
+
+        def there():
+            table_copy("core", j).wait()
+            table_copy("far", j).wait()
+
+        when(0, j, BLOCKS - 1 - lead, leave)
+        when(1, j, BLOCKS - lead, go_on)
+        when(lead, j, BLOCKS - 1, there)
+        for stage in range(6):
+
+            def advance(stage=stage):
+                if stage > 0:
+                    sums.take(stage - 1, ffn_group(j - 1 - stage))
+                sums.send(stage, ffn_group(j - 1 - stage))
+
+            when(1 + stage, j, BLOCKS - 1, advance)
+
+        def finished():
+            sums.take(5, ffn_group(j - 7))
+
+        when(7, j, BLOCKS - 1, finished)
+
+        base = ENDS_COLS + j * W_BLOCK
+        part = lambda place: pl.ds(pl.multiple_of(base + place * FB, 128), FB)
+        tab_gate, tab_up, tab_down = (tb_ref.at[:, part(place)] for place in range(3))
+        u = u_ref[...]
+        gate = dot(u, wg_ref[slot]) + dot(mg_ref[...], tab_gate[...])
+        up = dot(u, wu_ref[slot]) + dot(mu_ref[...], tab_up[...])
+        back = dot_nt(cot_ref[...], wd_ref[slot]) + dot(gd_ref[...], tab_down[...])
+        sig = jax.nn.sigmoid(gate)
+        silu = gate * sig
+        hidden = (silu * up).astype(bf16)
+        grad_gate = (back * up * sig * (1.0 + gate * (1.0 - sig))).astype(bf16)
+        grad_up = (back * silu).astype(bf16)
+        acc_ref[...] += dot(hidden, wd_ref[slot])
+        gn_ref[...] += dot_nt(grad_gate, wg_ref[slot]) + dot_nt(grad_up, wu_ref[slot])
+        dmid_ref[...] += dot_nt(hidden, tab_down[...])
+        gmg_ref[...] += dot_nt(grad_gate, tab_gate[...])
+        gmu_ref[...] += dot_nt(grad_up, tab_up[...])
+        put_grad(g_ref, part(0), dot_tn(mg_ref[...], grad_gate))
+        put_grad(g_ref, part(1), dot_tn(mu_ref[...], grad_up))
+        put_grad(g_ref, part(2), dot_tn(gd_ref[...], hidden))
+        return carry
+
+    lax.fori_loop(0, BLOCKS, block, 0)
+    dmid = (dmid_ref[...].astype(bf16).astype(f32) * twice).astype(bf16)
+    loads[2].wait()
+    for k in range(2):
+        cols = slice(512 * k, 512 * k + 512)
+        out_ref[:, cols] = (h1_ref[:, cols] + acc_ref[:, cols] + dot(dmid, b_down[:, cols])).astype(bf16)
+    put_grad(g_ref, slice(2 * D, 3 * D), dot_tn(dmid, cot_ref[...]))
+    gm_gate = (gmg_ref[...] * twice).astype(bf16)
+    gm_up = (gmu_ref[...] * twice).astype(bf16)
+    for k in range(2):
+        cols = slice(512 * k, 512 * k + 512)
+        gn_ref[:, cols] += dot(gm_gate, a_gate[:, cols]) + dot(gm_up, a_up[:, cols])
+    put_grad(g_ref, slice(0, D), dot_tn(gm_gate, u_ref[...]))
+    put_grad(g_ref, slice(D, 2 * D), dot_tn(gm_up, u_ref[...]))
+    for stage in range(6):
+        sums.take(stage, ffn_group(BLOCKS - 2 - stage))
+    stores = [
+        pltpu.make_async_copy(g_ref, g_hbm, load_sems.at[0]),
+        pltpu.make_async_copy(sum_ref, sum_hbm, load_sems.at[1]),
+    ]
+    for copy in stores:
+        copy.start()
+    for copy in stores:
+        copy.wait()
+
+
+def middle(seqs, length, *args):
+    rows = seqs * length
+    sd = jax.ShapeDtypeStruct
+    vm = pl.BlockSpec(memory_space=pltpu.VMEM)
+    hbm = pl.BlockSpec(memory_space=pl.ANY)
+    return pl.pallas_call(
+        functools.partial(middle_kernel, seqs, length),
+        in_specs=[vm] * 5 + [hbm] * 5,
+        out_specs=[vm, vm, hbm, hbm],
+        out_shape=[
+            sd((rows, D), bf16), sd((rows, D), f32), sd((2, 2, 32, FFN_COLS), bf16), sd((32, FFN_COLS), bf16),
+        ],
+        scratch_shapes=[
+            pltpu.VMEM((128, FFN_COLS), bf16),
+            pltpu.VMEM((2, D, FB), bf16),
+            pltpu.VMEM((2, D, FB), bf16),
+            pltpu.VMEM((2, FB, D), bf16),
+            pltpu.VMEM((rows, D), f32),
+            pltpu.VMEM((rows, D), f32),
+            pltpu.VMEM((rows, 128), f32),
+            pltpu.VMEM((rows, 128), f32),
+            pltpu.VMEM((rows, 128), f32),
+            pltpu.VMEM((rows, 128), bf16),
+            *sums_scratch(FFN_COLS),
+            pltpu.SemaphoreType.DMA((3,)),
+            pltpu.SemaphoreType.DMA((2, 3)),
+            pltpu.SemaphoreType.DMA((3 * BLOCKS,)),
+            pltpu.SemaphoreType.DMA((3 * BLOCKS,)),
+            pltpu.SemaphoreType.DMA((Sums.COPIES * BLOCKS,)),
+            pltpu.SemaphoreType.DMA((Sums.COPIES * BLOCKS,)),
+        ],
+        compiler_params=pltpu.CompilerParams(vmem_limit_bytes=60 * MIB, collective_id=3, has_side_effects=True),
+    )(*args)
+
+
+UPDATES = (
+    (B_GATE - D, D + FF), (B_UP - D, D + FF), (A_DOWN, FF + D), (A_OUT, 2 * D), (A_IN, 4 * D),
+)
+MOST = 2 * (D + FF) // 8
+NATIVE = tuple((2 * first // 8, 2 * count // 8) for first, count in UPDATES)
+
+
+def update_grad(na, part, sum_ref, lhs_ref, perm_ref, gn_ref):
+    first, count = UPDATES[part]
+    begin = na * first // 8
+    inside = lambda start: first <= start < first + count
+    chunks = [chunk for chunk in A_CHUNKS if inside(chunk[0])]
+    for n, (start, size) in enumerate(chunks):
+        for a in range(na):
+            row = (n * na + a) * RANK
+            if size < 1024:
+                lhs_ref[row : row + RANK, size:] = jnp.zeros((RANK, 1024 - size), bf16)
+            for k, col, breadth in a_pieces(start, size):
+                lhs_ref[row : row + RANK, k : k + breadth] = sum_ref[a * RANK : (a + 1) * RANK, col : col + breadth]
+    height = len(chunks) * na * RANK
+    full = dot_nt(lhs_ref[:height, :], perm_ref[...])
+    for n, (start, size) in enumerate(chunks):
+        for a in range(na):
+            row = (n * na + a) * RANK
+            turned = jnp.concatenate([full[row : row + RANK, 128 * c : 128 * c + 128] for c in range(8)], axis=0)
+            gn_ref[pl.ds(na * (start // 8) + a - begin, size // 8, stride=na), :] = turned.T[: size // 8]
+    for start, breadth in B_PARTS:
+        if inside(start):
+            blocks = breadth // 128
+            for a in range(na):
+                for c in range(blocks):
+                    col = wire(start, 128 * c)
+                    gn_ref[pl.ds(na * (start // 8 + c) + a - begin, RANK, stride=na * blocks), :] = sum_ref[
+                        a * RANK : (a + 1) * RANK, col : col + 128
+                    ].astype(f32)
+
+
+def finish_kernel(
+    seqs, length, count, na,
+    scal_ref, mask_ref, mo_ref, mi_ref, cw_ref, n1_ref, n2_ref,
+    tok_hbm, cot_hbm, h1_hbm, gn_hbm, gated_hbm, b_hbm, c_hbm, x_hbm, conv_hbm, same_hbm, u1_hbm,
+    tb_hbm, wi_hbm, wo_hbm, g_hbm, part_hbm, st_hbm, m_hbm, v_hbm,
+    ig_ref, new_hbm, all_hbm,
+    tok_ref, cot_ref, h1_ref, gn_ref, gated_ref, b_ref, c_ref, x_ref, conv_ref, same_ref, u1_ref,
+    tb_ref, wi_ref, wo_ref,
+    gh_ref, gb_ref, gg_ref, gp_ref, out_ref, in_ref,
+    g_ref, cr_ref, xr_ref, yr_ref, zr_ref, sum_ref,
+    lhs_ref, perm_ref, old_ref, grad_ref, new_ref, tab_ref,
+    halo_sems, load_sems, old_sems, new_sems, own_sems, spread_send, spread_recv, send_sems, recv_sems,
+):
+    at = Place()
+    seq = at.seq
+    met = announce(seq, count, [{"grp": at.core}, {"grp": at.gx}] + [{"seq": at.along_z(d)} for d in range(1, 4)])
+    ends = slice(W_ENDS, WIRE)
+    pairs = {
+        "h1": (h1_hbm, h1_ref), "gn": (gn_hbm, gn_ref), "cot": (cot_hbm, cot_ref),
+        "g": (g_hbm, g_ref.at[:, :, :, ends]),
+        "tb": (tb_hbm.at[:, :W_ENDS], tb_ref), "wo": (wo_hbm, wo_ref),
+        "c": (c_hbm, c_ref), "conv": (conv_hbm, conv_ref), "same": (same_hbm, same_ref.at[:, :, :length, :]),
+        "gated": (gated_hbm, gated_ref), "x": (x_hbm, x_ref), "b": (b_hbm, b_ref), "wi": (wi_hbm, wi_ref),
+        "u1": (u1_hbm, u1_ref), "tok": (tok_hbm, tok_ref),
+    }
+    sums = Sums(at, g_ref, cr_ref, xr_ref, yr_ref, zr_ref, sum_ref, send_sems, recv_sems)
+    every_row = slice(None)
+    for n, (rows, cols, shifted) in enumerate((
+        (every_row, pl.ds(W_FFN, 3 * W_BLOCK), pl.ds(ENDS_COLS, 3 * W_BLOCK)),
+        (every_row, *(sums.half(at.y, base + 3 * W_BLOCK, W_BLOCK) for base in (W_FFN, ENDS_COLS))),
+        (sums.unit(at.z, W_FFN, W_BLOCK)[0], *(sums.unit(at.z, base + 4 * W_BLOCK, W_BLOCK)[1] for base in (W_FFN, ENDS_COLS))),
+    )):
+        pairs["sum" + str(n)] = (part_hbm.at[rows, shifted], sum_ref.at[rows, cols])
+    names = list(pairs)
+
+    def load(*which):
+        return [pltpu.make_async_copy(*pairs[name], load_sems.at[names.index(name)]) for name in which]
+
+    def begin(*which):
+        for copy in load(*which):
+            copy.start()
+
+    def ready(*which):
+        for copy in load(*which):
+            copy.wait()
+
+    def old(part, slot):
+        first, size = NATIVE[part]
+        return [
+            pltpu.make_async_copy(ref.at[first : first + size], old_ref.at[slot, n, :size], old_sems.at[slot, n])
+            for n, ref in enumerate((st_hbm, m_hbm, v_hbm))
+        ]
+
+    begin("h1", "gn", "cot", "g", "sum0", "sum1", "sum2", "tb", "wo", "c", "conv", "same")
+    groups = {j: (j, W_FFN + j * W_BLOCK, W_BLOCK) for j in range(3, BLOCKS)}
+    groups["ends"] = (0, W_ENDS, W_FFN - W_ENDS)
+    groups["out"] = (1, W_B_C, W_ENDS - W_B_C)
+    groups["in"] = (2, 0, W_B_C)
+    following = {BLOCKS - 1 - stage: stage for stage in range(6)}
+    following["ends"] = 0
+
+    def step():
+        for name in list(following):
+            stage = following[name]
+            if stage > 0 and (isinstance(name, str) or stage > BLOCKS - 1 - name):
+                sums.take(stage - 1, groups[name])
+            if stage < 6:
+                sums.send(stage, groups[name])
+                following[name] = stage + 1
+            else:
+                del following[name]
+
+    own = lambda first, size: tab_ref.at[pl.ds(first, size), :]
+    slot_of = lambda owner, first, size: all_hbm.at[owner, pl.ds(first, size), :]
+    spread = Spread(at, own, slot_of, NATIVE, 16, spread_send, spread_recv)
+    going = {}
+
+    def pass_on():
+        for part in list(going):
+            spread.leg(going[part], part)
+            going[part] += 1
+            if going[part] > 5:
+                del going[part]
+
+    rate, inv = scal_ref[0], scal_ref[1]
+
+    def new_copy(part):
+        first, size = NATIVE[part]
+        return pltpu.make_async_copy(new_ref.at[part % 2, :size], new_hbm.at[first : first + size], new_sems.at[part % 2])
+
+    def own_copy(part):
+        first, size = NATIVE[part]
+        return pltpu.make_async_copy(
+            tab_ref.at[first : first + size], all_hbm.at[at.grp, first : first + size], own_sems.at[part]
+        )
+
+    def update(part):
+        first, size = NATIVE[part]
+        slot = part % 2
+        update_grad(na, part, sum_ref, lhs_ref, perm_ref, grad_ref)
+        for copy in old(part, slot):
+            copy.wait()
+        if part >= 2:
+            new_copy(part - 2).wait()
+        grad = grad_ref[:size]
+        one = 0.5 * old_ref[slot, 1, :size] + 0.5 * grad
+        two = 0.5 * old_ref[slot, 2, :size] + 0.5 * grad * grad
+        new = old_ref[slot, 0, :size] - rate * (one * inv) / (jnp.sqrt(two * inv) + 1e-08)
+        new_ref[slot, :size] = new
+        tab_ref[first : first + size] = new.astype(bf16)
+        new_copy(part).start()
+        own_copy(part).start()
+        if part + 2 < len(NATIVE):
+            for copy in old(part + 2, slot):
+                copy.start()
+        going[part] = 0
+
+    twice = 2.0 * row_mask(mask_ref, seqs, length)
+    ready("h1", "gn", "cot")
+    h1 = h1_ref[...]
+    inv2 = norm(h1, n2_ref[...])[1]
+    e2 = gn_ref[...] * n2_ref[...]
+    gh = cot_ref[...].astype(f32) + inv2 * e2 - h1 * (inv2 * inv2 * inv2 * jnp.mean(h1 * e2, axis=-1, keepdims=True))
+    gh_ref[...] = gh
+    gb_ref[...] = gh.astype(bf16)
+    begin("gated", "x", "b", "wi", "u1", "tok")
+    for part in range(2):
+        for copy in old(part, part):
+            copy.start()
+    ready("g", "sum0", "sum1", "sum2")
+    met()
+    step()
+    ready("tb", "wo")
+    gb = gb_ref[...]
+    gm_out = (dot_nt(gb, tb_ref[:, W_B_OUT : W_B_OUT + D]) * twice).astype(bf16)
+    for k in range(2):
+        cols = slice(512 * k, 512 * k + 512)
+        part = dot_nt(gb, wo_ref[cols, :]) + dot(gm_out, tb_ref[:, W_A_OUT + 512 * k : W_A_OUT + 512 * k + 512])
+        for s in range(seqs):
+            gg_ref[s, :length, cols] = part[s * length : (s + 1) * length, :]
+    step()
+    ready("c", "conv", "same")
+    for s in range(seqs):
+        rows = pl.ds(s * length, length)
+        gg = gg_ref[s, :length, :]
+        gp_ref[rows, D : 2 * D] = (gg * conv_ref[rows, :]).astype(bf16)
+        gg_ref[s, :length, :] = gg * c_ref[rows, :]
+        gg_ref[s, length:, :] = jnp.zeros((8, D), f32)
+        for k in range(2):
+            same_ref[k, s, length:, :] = jnp.zeros((8, 128), f32)
+        out_ref[2 * s : 2 * s + 1, :] = cw_ref[0:1, :] * same_ref[1, s, 0:1, 0:1] * gg_ref[s, 0:1, :]
+        out_ref[2 * s + 1 : 2 * s + 2, :] = (
+            cw_ref[0:1, :] * same_ref[1, s, 1:2, 0:1] * gg_ref[s, 1:2, :]
+            + cw_ref[1:2, :] * same_ref[0, s, 0:1, 0:1] * gg_ref[s, 0:1, :]
+        )
+    along = pltpu.make_async_remote_copy(
+        src_ref=out_ref, dst_ref=in_ref, send_sem=halo_sems.at[0], recv_sem=halo_sems.at[1],
+        device_id={"seq": seq - 1}, device_id_type=MESH,
+    )
+
+    @pl.when(seq > 0)
+    def _():
+        along.start()
+
+    ready("gated")
+    put_grad(g_ref, slice(W_A_OUT, W_A_OUT + D), dot_tn(gm_out, gated_ref[...]))
+    put_grad(g_ref, slice(W_B_OUT, W_B_OUT + D), dot_tn(mo_ref[...], gb))
+    put_grad(g_ref, slice(W_B_C, W_B_C + D), dot_tn(mi_ref[...], gp_ref[:, D : 2 * D]))
+    following["out"] = 0
+    step()
+
+    @pl.when(seq > 0)
+    def _():
+        along.wait_send()
+
+    @pl.when(seq < count - 1)
+    def _():
+        along.wait_recv()
+
+    ready("x", "b")
+    for s in range(seqs):
+        rows = pl.ds(s * length, length)
+        one, two = pl.ds(1, length), pl.ds(2, length)
+        gmix = (
+            cw_ref[2:3, :] * gg_ref[s, :length, :]
+            + cw_ref[1:2, :] * same_ref[0, s, one, 0:1] * gg_ref[s, one, :]
+            + cw_ref[0:1, :] * same_ref[1, s, two, 0:1] * gg_ref[s, two, :]
+        )
+        gg_ref[s, :length, :] = gmix
+
+    @pl.when(seq < count - 1)
+    def _():
+        for s in range(seqs):
+            gg_ref[s, length - 2 : length, :] += in_ref[2 * s : 2 * s + 2, :]
+
+    for s in range(seqs):
+        rows = pl.ds(s * length, length)
+        gmix = gg_ref[s, :length, :]
+        gp_ref[rows, 0:D] = (gmix * x_ref[rows, :]).astype(bf16)
+        gp_ref[rows, 2 * D :] = (gmix * b_ref[rows, :]).astype(bf16)
+    step()
+    gm_in = dot_nt(gp_ref[:, :D], tb_ref[:, W_B_B : W_B_B + D])
+    gm_in += dot_nt(gp_ref[:, D : 2 * D], tb_ref[:, W_B_C : W_B_C + D])
+    gm_in += dot_nt(gp_ref[:, 2 * D :], tb_ref[:, W_B_X : W_B_X + D])
+    gm_in = (gm_in * twice).astype(bf16)
+    ready("u1")
+    put_grad(g_ref, slice(W_B_B, W_B_B + D), dot_tn(mi_ref[...], gp_ref[:, :D]))
+    put_grad(g_ref, slice(W_B_X, W_B_X + D), dot_tn(mi_ref[...], gp_ref[:, 2 * D :]))
+    put_grad(g_ref, slice(W_A_IN, W_A_IN + D), dot_tn(gm_in, u1_ref[...]))
+    following["in"] = 0
+    step()
+    fill_shuffle(perm_ref)
+    ready("wi")
+    for k in range(4):
+        cols = slice(256 * k, 256 * k + 256)
+        gn_ref[:, cols] = dot_nt(gp_ref[...], wi_ref[cols, :]) + dot(gm_in, tb_ref[:, W_A_IN + 256 * k : W_A_IN + 256 * k + 256])
+        if k % 2 == 1:
+            step()
+    ready("tok")
+    tokens = tok_ref[...].astype(f32)
+    inv1 = norm(tokens, n1_ref[...])[1]
+    e1 = gn_ref[...] * n1_ref[...]
+    ig_ref[...] = (
+        gh_ref[...] + inv1 * e1 - tokens * (inv1 * inv1 * inv1 * jnp.mean(tokens * e1, axis=-1, keepdims=True))
+    ).astype(bf16)
+    for part in range(3):
+        while any(not isinstance(name, str) or name == "ends" for name in following):
+            step()
+        update(part)
+        pass_on()
+        step()
+    while following:
+        step()
+        pass_on()
+    for part in range(3, len(NATIVE)):
+        update(part)
+        pass_on()
+    while going:
+        pass_on()
+    for part in range(len(NATIVE)):
+        spread.sent(part)
+        own_copy(part).wait()
+    for part in range(len(NATIVE) - 2, len(NATIVE)):
+        new_copy(part).wait()
+
+
+def finish(seqs, length, count, na, *args):
+    rows = seqs * length
+    sd = jax.ShapeDtypeStruct
+    vm = pl.BlockSpec(memory_space=pltpu.VMEM)
+    hbm = pl.BlockSpec(memory_space=pl.ANY)
+    wide = pltpu.VMEM((rows, D), f32)
+    half = pltpu.VMEM((rows, D), bf16)
+    parts = len(NATIVE)
+    return pl.pallas_call(
+        functools.partial(finish_kernel, seqs, length, count, na),
+        in_specs=[pl.BlockSpec(memory_space=pltpu.SMEM)] + [vm] * 6 + [hbm] * 19,
+        out_specs=[vm, hbm, hbm],
+        out_shape=[sd((rows, D), bf16), sd((na * PACKROWS, 128), f32), sd((4, na * PACKROWS, 128), bf16)],
+        scratch_shapes=[
+            half, half, wide, wide, half, wide, wide, wide, wide, pltpu.VMEM((2, seqs, length + 8, 128), f32), half,
+            pltpu.VMEM((128, W_ENDS), bf16), pltpu.VMEM((D, 3 * D), bf16), pltpu.VMEM((D, D), bf16),
+            wide, half, pltpu.VMEM((seqs, length + 8, D), f32), pltpu.VMEM((rows, 3 * D), bf16),
+            pltpu.VMEM((2 * seqs, D), f32), pltpu.VMEM((2 * seqs, D), f32),
+            *sums_scratch(WIRE),
+            pltpu.VMEM((5 * na * RANK, 1024), bf16), pltpu.VMEM((1024, 1024), bf16),
+            pltpu.VMEM((2, 3, MOST, 128), f32), pltpu.VMEM((MOST, 128), f32), pltpu.VMEM((2, MOST, 128), f32),
+            pltpu.VMEM((na * PACKROWS, 128), bf16),
+            pltpu.SemaphoreType.DMA((2,)),
+            pltpu.SemaphoreType.DMA((18,)),
+            pltpu.SemaphoreType.DMA((2, 3)),
+            pltpu.SemaphoreType.DMA((2,)),
+            pltpu.SemaphoreType.DMA((parts,)),
+            pltpu.SemaphoreType.DMA((len(Spread.KINDS) * parts,)),
+            pltpu.SemaphoreType.DMA((len(Spread.KINDS) * parts,)),
+            pltpu.SemaphoreType.DMA((Sums.COPIES * BLOCKS,)),
+            pltpu.SemaphoreType.DMA((Sums.COPIES * BLOCKS,)),
+        ],
+        compiler_params=pltpu.CompilerParams(vmem_limit_bytes=63 * MIB, collective_id=4, has_side_effects=True),
+    )(*args)
+
+
+def lay_kernel(all_hbm, to_ref, all_ref, load_sems, store_sems):
+    cuts = 4
+    share = PACKROWS // cuts
+    parts = [(k, g, pl.ds(k * share, share)) for k in range(cuts) for g in range(4)]
+    loads = [pltpu.make_async_copy(all_hbm.at[g, rows], all_ref.at[g, rows], load_sems.at[k, g]) for k, g, rows in parts]
+    stores = [pltpu.make_async_copy(all_ref.at[g, rows], to_ref.at[rows, g], store_sems.at[k, g]) for k, g, rows in parts]
+    for copy in loads:
+        copy.start()
+    for came, goes in zip(loads, stores):
+        came.wait()
+        goes.start()
+    for copy in stores:
+        copy.wait()
+
+
+def lay_out(every, na):
+    hbm = pl.BlockSpec(memory_space=pl.ANY)
+    return pl.pallas_call(
+        lay_kernel,
+        in_specs=[hbm],
+        out_specs=hbm,
+        out_shape=jax.ShapeDtypeStruct((PACKROWS, 4, na, 128), bf16),
+        scratch_shapes=[
+            pltpu.VMEM((4, PACKROWS, na, 128), bf16),
+            pltpu.SemaphoreType.DMA((4, 4)),
+            pltpu.SemaphoreType.DMA((4, 4)),
+        ],
+        compiler_params=pltpu.CompilerParams(vmem_limit_bytes=60 * MIB),
+    )(every.reshape(4, PACKROWS, na, 128))
+
+
+def fast_device(
+    tokens, segment_ids, adapter_ids, input_weight, conv_weight, output_weight, gate_weight, up_weight, down_weight,
+    norm_one, norm_two, cotangent, adapter_state, first_moment, second_moment, rate, step,
+):
+    seqs, length, _ = tokens.shape
+    na = adapter_state.shape[0]
+    groups, count = lax.axis_size("grp"), lax.axis_size("seq")
+    native = lambda x: x.reshape(na, PACKROWS, 128).swapaxes(0, 1).reshape(na * PACKROWS, 128)
+    st, m, v = native(adapter_state), native(first_moment), native(second_moment)
+    adapters = na * groups
+    mask = (adapter_ids[:, None] == jnp.arange(adapters * RANK, dtype=jnp.int32)[None, :] // RANK).astype(f32)
+    ids = segment_ids.astype(f32)
+    rows = seqs * length
+    tok2, cot2 = tokens.reshape(rows, D), cotangent.reshape(rows, D)
+    n1, n2 = norm_one.reshape(1, D), norm_two.reshape(1, D)
+    table, u1, mi, b, c, x, conv, same, gated, mo, h1, u2, mg, mu = start(
+        seqs, length, count, na, st, tok2, ids, mask, input_weight, conv_weight, output_weight, n1, n2
+    )
+    out, gn, grads, sums = middle(
+        seqs, length, u2, cot2, mg, mu, mask, h1, gate_weight, up_weight, down_weight, table
+    )
+    correction = 1.0 - jnp.power(jnp.float32(0.5), step[0].astype(f32))
+    scal = jnp.stack([rate[0], 1.0 / correction])
+    ig, new, every = finish(
+        seqs, length, count, na, scal, mask, mo, mi, conv_weight, n1, n2,
+        tok2, cot2, h1, gn, gated, b, c, x, conv, same.reshape(2, seqs, length, 128), u1,
+        table, input_weight, output_weight, grads, sums, st, m, v,
+    )
+    every = lay_out(every, na).reshape(PACKROWS, adapters, 128).swapaxes(0, 1).reshape(adapters, PACKROWS * 128)
     new = new.reshape(PACKROWS, na, 128).swapaxes(0, 1).reshape(na, PACKROWS * 128)
     return out.reshape(tokens.shape), ig.reshape(tokens.shape), new, every
 
@@ -476,7 +1477,7 @@
     rows = P("grp", "seq", None)
     own = P("grp", None)
     return jax.shard_map(
-        per_device,
+        fast_device if tuple(mesh.shape[axis] for axis in ("seq", "grp")) == (8, 4) else general_device,
         mesh=mesh,
         in_specs=(rows, P("grp", "seq"), P("grp")) + (P(),) * 8 + (rows, own, own, own, P(), P()),
         out_specs=(rows, rows, own, P()),

time: 471 us -> 180 us (0.38)
  waiting for transfers between devices: 306 us -> 0 us
  Pallas kernels: 110 us -> 170 us
  local copies, waits for them, and re-layouts: 30.8 us -> 4.18 us
  between operations: 15.4 us -> 2.07 us
    psum x1 -> x0, waiting for transfers between devices: 125 us -> none  [per_device(): lax.psum(lax.psum_scatter(grads, 'grp', scatter_dimension=0, tiled=True),...]
    reduce_scatter x1 -> x0, waiting for transfers between devices: 92.2 us -> none  [per_device(): lax.psum_scatter(grads, 'grp', scatter_dimension=0, tiled=True)]
    all_gather x2 -> x0, waiting for transfers between devices: 89 us -> none  [the longest x1 45.7 us: per_device(): table = lax.all_gather(own, 'grp', axis=0, tiled=True)]
    pallas_call x5 -> x4, Pallas kernels: 110 us -> 170 us  [the longest x1 74.3 us: finish(): pl.pallas_call(functools.partial(finish_kernel, seqs, length, count, na),...]
    unnamed x31 -> x9, local copies, waits for them, and re-layouts: 25.4 us -> 4.18 us
  transfers between devices with their start and end apart: 4 -> 0, of which waited for: 4 -> 0; matrix products, arithmetic and copies ran while one was open for 0% -> 0% of each run, Pallas kernels for 0% -> 0%
where the time goes in v2:
time: 180 us; the launch traced here: 179 us
  Pallas kernels  170 us (94%)
  local copies, waits for them, and re-layouts  4.18 us (2%)
  other arithmetic  3.15 us (2%)
  between operations  2.07 us (1%)
    pallas_call x1, Pallas kernels, finish(): pl.pallas_call(functools.partial(finish_kernel, seqs, length, count, na),...  74.3 us
    pallas_call x1, Pallas kernels, middle(): pl.pallas_call(functools.partial(middle_kernel, seqs, length), in_specs=[...  60.7 us
    pallas_call x1, Pallas kernels, start(): pl.pallas_call(functools.partial(start_kernel, seqs, length, count, na),...  29.5 us
    pallas_call x1, Pallas kernels, lay_out(): pl.pallas_call(lay_kernel, in_specs=[hbm], out_specs=hbm, out_shape=jax.S...  5.41 us
    unnamed x9, local copies, waits for them, and re-layouts  4.18 us

profile of v2, /device:TPU:0, one launch (start us, length us, event | category | flops | bytes accessed | tf_op | source)
XLA Modules:
  0.0 179.3 jit_solution(16883896509105099108)
XLA Ops:
  0.6 1.3 convert_element_type.10.ids_ref
  1.9 1.3 compare_convert_fusion.mask_ref
  3.2 29.5 %shard_map.192 = (bf16[128,23040]{1,0:T(8,128)(2,1)}, bf16[512,1024]{1,0:T(8,128)(2,1)}, bf16[512,128]{1,0:T(8,128)(2,1)}, f32[512,1024]{1,0:T(8,128)}, f32[512,...) custom-call(f32[5760,128]{1,0:T(8,128)} %bitcast.33, ...), custom_call_target="tpu_custom_call" | custom-call | tf_op jit(solution)/shard_map/pallas_call | solution.py:774
  32.7 60.7 %shard_map.193 = (bf16[512,1024]{1,0:T(8,128)(2,1)}, f32[512,1024]{1,0:T(8,128)}, bf16[2,2,32,16896]{3,2,1,0:T(8,128)(2,1)}, bf16[32,16896]{1,0:T(8,128)(2,1)}) custom-call(bf16[512,1024]{1,0:T(8,128)(2,1)} %get-tuple-element.25.u_ref, bf16[512,1024]{1,0:T(8,128)(2,1)} %bitcast.39, bf16[512,128]{1,0:T(8,128)(2,1)} %get-tuple-element.26.mg_ref, ...), custom_call_target="tpu_custom_call" | custom-call | tf_op jit(solution)/shard_map/pallas_call | solution.py:1063
  94.8 0.6 pad_maximum_fusion.scal_ref
  95.4 74.3 %shard_map.194 = (bf16[512,1024]{1,0:T(8,128)(2,1)}, f32[5760,128]{1,0:T(8,128)}, bf16[4,5760,128]{2,1,0:T(8,128)(2,1)}) custom-call(f32[2]{0:T(128)} %pad_maximum_fusion.scal_ref, f32[4,128]{1,0:T(4,128)} %compare_convert_fusion.mask_ref, bf16[512,128]{1,0:T(8,128)(2,1)} %get-tuple-element.31.mo_ref, bf16[512,128]{1,0:T(8,128)(2,1)} %get-tuple-element.32.mi_ref, ...), custom_call_target="tpu_custom_call" | custom-call | tf_op jit(solution)/shard_map/pallas_call | solution.py:1384
  169.7 0.0 copy-start.1
  169.7 0.0 copy-start.2
  169.7 5.4 %shard_map.195 = bf16[2880,4,2,128]{3,2,1,0:T(2,128)(2,1)} custom-call(bf16[4,2880,2,128]{3,2,1,0:T(2,128)(2,1)} %bitcast.36), custom_call_target="tpu_custom_call" | custom-call | tf_op jit(solution)/shard_map/pallas_call | solution.py:1429
  175.1 0.0 copy-start
  175.1 0.0 copy-done.1
  175.1 1.0 copy.30
  176.1 0.0 copy-done.2
  176.1 1.0 copy.31
  177.1 0.6 copy-done
  177.7 1.6 copy.32
  (1 shorter events, 0.0 us)
Async XLA Ops:
  169.7 5.4 %copy-start.1 = (bf16[512,1024]{1,0:T(8,128)(2,1)S(1)}, bf16[512,1024]{1,0:T(8,128)(2,1)}, u32[]{:S(2)}) copy-start(bf16[512,1024]{1,0:T(8,128)(2,1)} %get-tuple-element.30) | copy-start | bytes 3145732
  169.7 6.4 %copy-start.2 = (bf16[512,1024]{1,0:T(8,128)(2,1)S(1)}, bf16[512,1024]{1,0:T(8,128)(2,1)}, u32[]{:S(2)}) copy-start(bf16[512,1024]{1,0:T(8,128)(2,1)} %get-tuple-element.43) | copy-start | bytes 3145732
  175.1 2.6 %copy-start = (f32[5760,128]{1,0:T(8,128)S(1)}, f32[5760,128]{1,0:T(8,128)}, u32[]{:S(2)}) copy-start(f32[5760,128]{1,0:T(8,128)} %get-tuple-element.44) | copy-start | bytes 8847364
